TPU v7x, 32 devices: a whole 2x2x4 slice. The times are simulated.
32 devices in a mesh: box: 8 (over z, x), dir: 4 (over y, core).
Axes of the slice: x: 2, y: 2, z: 4, core: 2. Of those that a mesh axis runs over, the one named last changes fastest.
Arguments:
- currents: bfloat16 [2, 768, 128, 256], P(None, ('box', 'dir')), may hold values from -6 to 6
- near_tiles: bfloat16 [768, 9, 2, 128, 128], P(('box', 'dir')), may hold values from -0.125 to 0.125
- near_index: int32 [768, 9], P(('box', 'dir')), may hold values from 0 to 767, as said below
- near_count: int32 [768], P(('box', 'dir')), may hold values from 2 to 9
- radiate: bfloat16 [768, 2, 128, 128], P(('box', 'dir')), may hold values from -0.375 to 0.375
- receive: bfloat16 [768, 2, 128, 128], P(('box', 'dir')), may hold values from -0.375 to 0.375
- interp: bfloat16 [512, 128], replicated, may hold values from -0.1875 to 0.1875
- shift_angle: float32 [8, 512], replicated, may hold values from -3.140625 to 3.140625
- far_index: int32 [96, 48], replicated, may hold values from 0 to 95, as said below
- far_count: int32 [96], replicated, may hold values from 12 to 48
- trans_index: int32 [96, 48], replicated, may hold values from 0 to 315
- translators: float32 [316, 2, 512], P(None, None, ('box', 'dir')), may hold values from -0.625 to 0.625
Outputs:
- response: bfloat16 [2, 768, 128, 256], P(None, ('box', 'dir'))
Inputs may be any that keep to these rules, and one draw needn't show every extreme that they name: `near_index`: slot 0 of box b is b itself; every entry lies within 12 of its own box's index. `far_index`: no parent box lists itself.
All inputs are finite; a program needn't handle non-finite values.
Results may differ from a plain program's by a relative error of at most 0.007.
Values may be sent and summed in bfloat16 or wider, within the bound.
A program may use at most 256 MiB of HBM per device.

v0:
```python
import jax
import jax.numpy as jnp
from jax import lax
from jax.experimental import pallas as pl
from jax.experimental.pallas import tpu as pltpu
from jax.sharding import PartitionSpec as P

AXES = ("box", "dir")
VMEM_BYTES = 48 * 1024 * 1024


def passed_along(value, axis, by):
    peers = lax.axis_size(axis)
    pairs = [(i, i + by) for i in range(peers) if 0 <= i + by < peers]
    return lax.ppermute(value, axis, pairs)


def complex_matrix(real, imag):
    top = jnp.concatenate([real, -imag], axis=1)
    bottom = jnp.concatenate([imag, real], axis=1)
    return jnp.concatenate([top, bottom], axis=0)


def dot(left, right):
    return jnp.dot(left, right, preferred_element_type=jnp.float32)


def upward(currents, radiate, interp, cosine, sine, parts):
    _, boxes, unknowns, columns = currents.shape
    parents = boxes // 8
    directions, leaf_dirs = interp.shape
    share = directions // parts
    half = directions // 2
    split = share % 16 == 0
    width = 2 * leaf_dirs
    currents = currents.reshape(2, parents, 8, unknowns, columns)
    radiate = radiate.reshape(parents, 8, 2, leaf_dirs, unknowns)

    def body(cur_ref, rad_ref, interp_ref, cos_ref, sin_ref, out_ref, leaf_ref, shift_ref):
        step = pl.program_id(0)

        @pl.when(step == 0)
        def _():
            wide = interp_ref[...].astype(jnp.float32)
            for c in range(8):
                real = (wide * cos_ref[:, c : c + 1]).astype(jnp.bfloat16)
                imag = (wide * sin_ref[:, c : c + 1]).astype(jnp.bfloat16)
                shift_ref[c] = complex_matrix(real, imag)

        @pl.when(step < 8)
        def _():
            rows = pl.ds(pl.multiple_of(step * width, width), width)
            for parent in range(parents):
                mat = complex_matrix(rad_ref[parent, 0, 0], rad_ref[parent, 0, 1])
                vec = jnp.concatenate([cur_ref[0, parent, 0], cur_ref[1, parent, 0]], axis=0)
                leaf = dot(mat, vec).astype(jnp.bfloat16)
                leaf_ref[rows, parent * columns : (parent + 1) * columns] = leaf
        @pl.when(step >= 8)
        def _():
            quarter = step - 8
            rows = pl.ds(pl.multiple_of(quarter * half, half), half)
            mat = jnp.concatenate([shift_ref[c, rows, :] for c in range(8)], axis=1)
            result = dot(mat, leaf_ref[...]).astype(jnp.bfloat16)
            for parent in range(parents):
                piece = result[:, parent * columns : (parent + 1) * columns]
                if split:
                    out_ref[:, 0, parent] = piece.reshape(half // share, share, columns)
                else:
                    out_ref[0, parent] = piece

    def early(i):
        return jnp.minimum(i, 7)

    def late(i):
        return jnp.maximum(i - 8, 0)

    if split:
        out_shape = (parts, 2, parents, share, columns)
        out_spec = pl.BlockSpec(
            (parts // 2, 1, parents, share, columns),
            lambda i: (late(i) % 2, late(i) // 2, 0, 0, 0),
        )
    else:
        out_shape = (2, parents, directions, columns)
        out_spec = pl.BlockSpec(
            (1, parents, half, columns), lambda i: (late(i) // 2, 0, late(i) % 2, 0)
        )
    out = pl.pallas_call(
        body,
        grid=(12,),
        in_specs=[
            pl.BlockSpec((2, parents, 1, unknowns, columns), lambda i: (0, 0, early(i), 0, 0)),
            pl.BlockSpec((parents, 1, 2, leaf_dirs, unknowns), lambda i: (0, early(i), 0, 0, 0)),
            pl.BlockSpec((directions, leaf_dirs), lambda i: (0, 0)),
            pl.BlockSpec((directions, 8), lambda i: (0, 0)),
            pl.BlockSpec((directions, 8), lambda i: (0, 0)),
        ],
        out_specs=out_spec,
        out_shape=jax.ShapeDtypeStruct(out_shape, jnp.bfloat16),
        scratch_shapes=[
            pltpu.VMEM((8 * width, parents * columns), jnp.bfloat16),
            pltpu.VMEM((8, 2 * directions, width), jnp.bfloat16),
        ],
        compiler_params=pltpu.CompilerParams(vmem_limit_bytes=VMEM_BYTES),
        name="upward",
    )(currents, radiate, interp, cosine.T, sine.T)
    if not split:
        out = out.reshape(2, parents, parts, share, columns)
        out = jnp.transpose(out, (2, 0, 1, 3, 4))
    return out


def near_products(lower, currents, upper, near_tiles, near_index, near_count, first):
    _, boxes, unknowns, columns = currents.shape
    reach = boxes // 2
    slots = near_tiles.shape[1]

    def body(index_ref, count_ref, low_ref, cur_ref, up_ref, tile_ref, out_ref, window, acc, sems):
        box = pl.program_id(0)

        @pl.when(box == 0)
        def _():
            copies = []
            for part in range(2):
                rows = pl.ds(part * unknowns, unknowns)
                for order, (ref, start, size) in enumerate(
                    ((low_ref, 0, reach), (cur_ref, reach, boxes), (up_ref, reach + boxes, reach))
                ):
                    copies.append(
                        pltpu.make_async_copy(
                            ref.at[part],
                            window.at[pl.ds(start, size), rows],
                            sems.at[3 * part + order],
                        )
                    )
            for copy in copies:
                copy.start()
            for copy in copies:
                copy.wait()

        def product(slot):
            mat = complex_matrix(tile_ref[0, slot, 0], tile_ref[0, slot, 1])
            return dot(mat, window[index_ref[box * slots + slot]])

        acc[...] = product(0) + product(1)

        def add(slot, carry):
            acc[...] += product(slot)
            return carry

        lax.fori_loop(2, count_ref[box], add, 0)
        total = acc[...].astype(jnp.bfloat16)
        out_ref[0, 0] = total[:unknowns]
        out_ref[1, 0] = total[unknowns:]

    local_index = jnp.clip(near_index - first, 0, 2 * boxes - 1).reshape(-1)
    flops = boxes * slots * 8 * unknowns * unknowns * columns
    return pl.pallas_call(
        body,
        grid_spec=pltpu.PrefetchScalarGridSpec(
            num_scalar_prefetch=2,
            grid=(boxes,),
            in_specs=[
                pl.BlockSpec(memory_space=pl.ANY),
                pl.BlockSpec(memory_space=pl.ANY),
                pl.BlockSpec(memory_space=pl.ANY),
                pl.BlockSpec(
                    (1, slots, 2, unknowns, unknowns), lambda b, index, count: (b, 0, 0, 0, 0)
                ),
            ],
            out_specs=pl.BlockSpec(
                (2, 1, unknowns, columns), lambda b, index, count: (0, b, 0, 0)
            ),
            scratch_shapes=[
                pltpu.VMEM((2 * boxes, 2 * unknowns, columns), jnp.bfloat16),
                pltpu.VMEM((2 * unknowns, columns), jnp.float32),
                pltpu.SemaphoreType.DMA((6,)),
            ],
        ),
        out_shape=jax.ShapeDtypeStruct(currents.shape, jnp.bfloat16),
        compiler_params=pltpu.CompilerParams(vmem_limit_bytes=VMEM_BYTES),
        cost_estimate=pl.CostEstimate(
            flops=flops,
            bytes_accessed=2 * near_tiles.size + 8 * currents.size,
            transcendentals=0,
        ),
        name="near_products",
    )(local_index, near_count, lower, currents, upper, near_tiles)


def translation_matrix(far_index, far_count, trans_index, translators):
    parent_total, slot_count = far_index.shape
    operators, _, share = translators.shape
    slot_ids = jnp.arange(slot_count, dtype=jnp.int32)
    live = slot_ids[None, :] < far_count[:, None]
    chosen = jnp.where(live, trans_index, -1).reshape(-1)
    pick = (chosen[:, None] == jnp.arange(operators, dtype=jnp.int32)[None, :]).astype(jnp.bfloat16)
    table = translators.reshape(operators, 2 * share)
    factor = dot(pick, table.astype(jnp.bfloat16)).astype(jnp.bfloat16)
    factor = factor.reshape(parent_total, slot_count, 2 * share)
    parent_ids = jnp.arange(parent_total, dtype=jnp.int32)
    selector = (far_index[:, :, None] == parent_ids[None, None, :]).astype(jnp.bfloat16)
    matrix = jnp.einsum("psx,psq->xpq", factor, selector, preferred_element_type=jnp.float32)
    return matrix.astype(jnp.bfloat16)


def wire_matrix(matrix, parts):
    share = matrix.shape[0] // 2
    total = matrix.shape[1]
    each = total // parts
    place = jnp.arange(2 * total, dtype=jnp.int32)
    parent = place // (2 * each) * each + place % each
    same = parent[:, None] == jnp.arange(total, dtype=jnp.int32)[None, :]
    part = place // each % 2
    spread = jnp.stack([same & (part == c)[:, None] for c in range(2)]).astype(jnp.bfloat16)
    gather = jnp.transpose(spread, (0, 2, 1))

    def body(real_ref, imag_ref, spread_ref, gather_ref, out_ref):
        real = real_ref[0]
        imag = imag_ref[0]
        top = dot(real, gather_ref[0]) - dot(imag, gather_ref[1])
        bottom = dot(imag, gather_ref[0]) + dot(real, gather_ref[1])
        result = dot(spread_ref[0], top.astype(jnp.bfloat16))
        result = result + dot(spread_ref[1], bottom.astype(jnp.bfloat16))
        out_ref[0] = result.astype(jnp.bfloat16)

    return pl.pallas_call(
        body,
        grid=(share,),
        in_specs=[
            pl.BlockSpec((1, total, total), lambda j: (j, 0, 0)),
            pl.BlockSpec((1, total, total), lambda j: (share + j, 0, 0)),
            pl.BlockSpec((2, 2 * total, total), lambda j: (0, 0, 0)),
            pl.BlockSpec((2, total, 2 * total), lambda j: (0, 0, 0)),
        ],
        out_specs=pl.BlockSpec((1, 2 * total, 2 * total), lambda j: (j, 0, 0)),
        out_shape=jax.ShapeDtypeStruct((share, 2 * total, 2 * total), jnp.bfloat16),
        compiler_params=pltpu.CompilerParams(vmem_limit_bytes=VMEM_BYTES),
        cost_estimate=pl.CostEstimate(
            flops=16 * share * total**3, bytes_accessed=12 * share * total**2, transcendentals=0
        ),
        name="wire_matrix",
    )(matrix, matrix, spread, gather)


def translate(patterns, matrix):
    parts, _, parents, share, columns = patterns.shape
    rows = parts * 2 * parents
    half = columns // 2

    def body(in_ref, mat_ref, out_ref, wide, result):
        wide[...] = in_ref[...].astype(jnp.float32)

        for j in range(share):
            source = wide[pl.ds(j, rows, stride=share), :].astype(jnp.bfloat16)
            result[pl.ds(j, rows, stride=share), :] = dot(mat_ref[j], source)
        out_ref[...] = result[...].astype(jnp.bfloat16)

    out = pl.pallas_call(
        body,
        grid=(columns // half,),
        in_specs=[
            pl.BlockSpec((rows * share, half), lambda i: (0, i)),
            pl.BlockSpec((share, rows, rows), lambda i: (0, 0, 0)),
        ],
        out_specs=pl.BlockSpec((rows * share, half), lambda i: (0, i)),
        out_shape=jax.ShapeDtypeStruct((rows * share, columns), jnp.bfloat16),
        scratch_shapes=[
            pltpu.VMEM((rows * share, half), jnp.float32),
            pltpu.VMEM((rows * share, half), jnp.float32),
        ],
        compiler_params=pltpu.CompilerParams(vmem_limit_bytes=VMEM_BYTES),
        name="translate",
    )(patterns.reshape(rows * share, columns), matrix)
    return out.reshape(patterns.shape)


def downward(incoming, near, receive, interp_t, cosine, sine):
    parts, _, parents, share, columns = incoming.shape
    _, boxes, unknowns, _ = near.shape
    leaf_dirs, directions = interp_t.shape
    split = share % 16 == 0
    near = near.reshape(2, parents, 8, unknowns, columns)
    receive = receive.reshape(parents, 8, 2, unknowns, leaf_dirs)
    if not split:
        incoming = jnp.transpose(incoming, (1, 2, 0, 3, 4)).reshape(2, parents, directions, columns)

    def body(in_ref, near_ref, rec_ref, interp_ref, cos_ref, sin_ref, out_ref, source):
        @pl.when(pl.program_id(0) == 0)
        def _():
            for part in range(2):
                for parent in range(parents):
                    if split:
                        piece = in_ref[:, part, parent].reshape(directions, columns)
                    else:
                        piece = in_ref[part, parent]
                    source[
                        part * directions : (part + 1) * directions,
                        parent * columns : (parent + 1) * columns,
                    ] = piece

        wide = interp_ref[...].astype(jnp.float32)
        real = (wide * cos_ref[0]).astype(jnp.bfloat16)
        imag = (wide * sin_ref[0]).astype(jnp.bfloat16)
        arriving = dot(complex_matrix(real, -imag), source[...]).astype(jnp.bfloat16)
        for parent in range(parents):
            mat = complex_matrix(rec_ref[parent, 0, 0], rec_ref[parent, 0, 1])
            far = dot(mat, arriving[:, parent * columns : (parent + 1) * columns])
            for part in range(2):
                total = near_ref[part, parent, 0].astype(jnp.float32)
                total = total + far[part * unknowns : (part + 1) * unknowns]
                out_ref[part, parent, 0] = total.astype(jnp.bfloat16)

    whole = (0,) * incoming.ndim
    out = pl.pallas_call(
        body,
        grid=(8,),
        in_specs=[
            pl.BlockSpec(incoming.shape, lambda i: whole),
            pl.BlockSpec((2, parents, 1, unknowns, columns), lambda i: (0, 0, i, 0, 0)),
            pl.BlockSpec((parents, 1, 2, unknowns, leaf_dirs), lambda i: (0, i, 0, 0, 0)),
            pl.BlockSpec((leaf_dirs, directions), lambda i: (0, 0)),
            pl.BlockSpec((1, 1, directions), lambda i: (i, 0, 0)),
            pl.BlockSpec((1, 1, directions), lambda i: (i, 0, 0)),
        ],
        out_specs=pl.BlockSpec((2, parents, 1, unknowns, columns), lambda i: (0, 0, i, 0, 0)),
        out_shape=jax.ShapeDtypeStruct(near.shape, jnp.bfloat16),
        scratch_shapes=[pltpu.VMEM((2 * directions, parents * columns), jnp.bfloat16)],
        compiler_params=pltpu.CompilerParams(vmem_limit_bytes=VMEM_BYTES),
        name="downward",
    )(incoming, near, receive, interp_t, cosine[:, None, :], sine[:, None, :])
    return out.reshape(2, boxes, unknowns, columns)


def local(
    currents,
    near_tiles,
    near_index,
    near_count,
    radiate,
    receive,
    interp,
    shift_angle,
    far_index,
    far_count,
    trans_index,
    translators,
):
    boxes = currents.shape[1]
    reach = boxes // 2
    parts = lax.axis_size(AXES)
    lower = passed_along(currents[:, boxes - reach :], AXES, 1)
    upper = passed_along(currents[:, :reach], AXES, -1)
    cosine = jnp.cos(shift_angle)
    sine = jnp.sin(shift_angle)
    parent = upward(currents, radiate, interp, cosine, sine, parts)
    parent, near_count, far_index, trans_index, translators = lax.optimization_barrier(
        (parent, near_count, far_index, trans_index, translators)
    )
    by_direction = lax.all_to_all(parent, AXES, split_axis=0, concat_axis=0, tiled=True)
    matrix = wire_matrix(
        translation_matrix(far_index, far_count, trans_index, translators), parts
    )
    first = lax.axis_index(AXES) * boxes - reach
    near = near_products(lower, currents, upper, near_tiles, near_index, near_count, first)
    translated = translate(by_direction, matrix)
    incoming = lax.all_to_all(translated, AXES, split_axis=0, concat_axis=0, tiled=True)
    return downward(incoming, near, receive, interp.T, cosine, sine)


def solution(mesh):
    placed = (
        P(None, ("box", "dir"), None, None),
        P(("box", "dir"), None, None, None, None),
        P(("box", "dir"), None),
        P(("box", "dir")),
        P(("box", "dir"), None, None, None),
        P(("box", "dir"), None, None, None),
        P(),
        P(),
        P(),
        P(),
        P(),
        P(None, None, ("box", "dir")),
    )
    return jax.shard_map(
        local,
        mesh=mesh,
        in_specs=placed,
        out_specs=P(None, ("box", "dir"), None, None),
        check_vma=False,
    )
```

profile of v0, /device:TPU:25, one launch (start us, length us, event | category | flops | bytes accessed | tf_op | source)
XLA Modules:
  0.0 165.6 jit_solution(14903295316712426202)
XLA Ops:
  0.0 0.8 fusion.18
  0.8 0.1 copy.29.cos_ref
  0.9 0.1 copy.30.sin_ref
  1.1 0.0 copy-start.3
  1.1 1.4 copy-done.3
  2.5 0.0 copy-start.4
  2.5 0.9 copy-done.4
  3.4 11.6 %upward.1 = bf16[32,2,3,16,256]{4,3,2,1,0:T(8,128)(2,1)} custom-call(bf16[2,3,8,128,256]{4,3,2,1,0:T(8,128)(2,1)} %bitcast.25, bf16[3,8,2,128,128]{4,3,2,1,0:T(8,128)(2,1)S(1)} %bitcast.23, bf16[512,128]{1,0:T(8,128)(2,1)S(1)} %copy-done.4, f32[512,8]{1,0:T(8,128)S(1)} %copy.29.cos_ref, f32[512,8]{1,0:T(8,128)S(1)} %copy.30.sin_ref), custom_call_target="tpu_custom_call" | custom-call | tf_op jit(solution)/shard_map/upward/pallas_call | solution.py:88
  15.0 6.2 %all-to-all-start = ((bf16[32,2,3,16,256]{4,3,2,1,0:T(8,128)(2,1)}), bf16[32,2,3,16,256]{4,3,2,1,0:T(8,128)(2,1)S(1)}, u32[]{:S(2)}, u32[]{:S(2)}) async-start(bf16[32,2,3,16,256]{4,3,2,1,0:T(8,128)(2,1)} %upward.1), calls=%async_computation | async-start | bytes 3145728 | tf_op jit(solution)/shard_map/all_to_all | solution.py:360
  21.2 0.0 copy-done.8
  21.2 0.0 copy-done.11
  21.2 0.0 copy-start.9
  21.3 0.1 copy.32
  21.4 0.1 eq.80
  21.5 0.0 copy-done.7
  21.5 1.1 fusion.1
  22.6 0.8 reshape.177
  23.4 0.0 copy-done.9
  23.4 0.1 copy.31
  23.5 1.5 fusion.3
  25.0 0.3 copy.43
  25.4 0.1 copy.35.spread_ref
  25.5 7.2 %wire_matrix.1.mat_ref = bf16[16,192,192]{2,1,0:T(8,128)(2,1)S(1)} custom-call(bf16[32,96,96]{2,1,0:T(8,128)(2,1)S(1)} %bitcast.19, bf16[32,96,96]{2,1,0:T(8,128)(2,1)S(1)} %bitcast.20, bf16[2,192,96]{2,1,0:T(8,128)(2,1)S(1)} %copy.35.spread_ref, bf16[2,96,192]{2,1,0:T(8,128)(2,1)S(1)} %get-tuple-element.17.gather_ref), custom_call_target="tpu_custom_call" | custom-call | flops 226492416 | bytes 1769472 | tf_op jit(solution)/shard_map/wire_matrix/pallas_call | solution.py:227
  32.7 0.0 copy-start
  32.7 1.2 copy-done
  33.9 22.6 %all-to-all-done = bf16[32,2,3,16,256]{4,3,2,1,0:T(8,128)(2,1)S(1)} async-done(((bf16[32,2,3,16,256]{4,3,2,1,0:T(8,128)(2,1)}), bf16[32,2,3,16,256]{4,3,2,1,0:T(8,128)(2,1)S(1)}, u32[]{:S(2)}, u32[]{:S(2)}) %all-to-all-start) | async-done | bytes 1572896 | tf_op jit(solution)/shard_map/all_to_all | solution.py:360
  56.5 1.4 copy-done.1
  57.9 3.5 %translate.1 = bf16[3072,256]{1,0:T(8,128)(2,1)} custom-call(bf16[3072,256]{1,0:T(8,128)(2,1)S(1)} %bitcast.21, bf16[16,192,192]{2,1,0:T(8,128)(2,1)S(1)} %copy-done.1), custom_call_target="tpu_custom_call" | custom-call | tf_op jit(solution)/shard_map/translate/pallas_call | solution.py:259
  61.4 5.9 %all-to-all-start.1 = ((bf16[32,2,3,16,256]{4,3,2,1,0:T(8,128)(2,1)}), bf16[32,2,3,16,256]{4,3,2,1,0:T(8,128)(2,1)S(1)}, u32[]{:S(2)}, u32[]{:S(2)}) async-start(bf16[32,2,3,16,256]{4,3,2,1,0:T(8,128)(2,1)} %bitcast.8), calls=%async_computation.1 | async-start | bytes 3145728 | tf_op jit(solution)/shard_map/all_to_all | solution.py:367
  67.4 0.0 copy-start.5
  67.4 0.0 copy-start.10
  67.4 0.0 copy-start.6
  67.4 3.9 %fusion.17 = (bf16[2,12,128,256]{3,2,1,0:T(8,128)(2,1)}, bf16[2,12,128,256]{3,2,1,0:T(8,128)(2,1)}) fusion(bf16[2,24,128,256]{3,2,1,0:T(8,128)(2,1)} %cur_ref.1), kind=kLoop, calls=%fused_computation.36 | loop fusion | bytes 6291456 | tf_op jit(solution)/shard_map/slice | solution.py:353
  71.3 3.4 %collective-permute-start = (bf16[2,12,128,256]{3,2,1,0:T(8,128)(2,1)}, bf16[2,12,128,256]{3,2,1,0:T(8,128)(2,1)}, u32[]{:S(2)}, u32[]{:S(2)}) collective-permute-start(bf16[2,12,128,256]{3,2,1,0:T(8,128)(2,1)} %get-tuple-element.16), channel_id=1, source_target_pairs={{0,1},{1,2},{2,3},{3,4},{4,5},{5,6},{6,7},{7,8},{8,9},{9,10},{10,1... | collective-permute-start | bytes 4718600 | tf_op jit(solution)/shard_map/ppermute | solution.py:15
  74.7 1.9 %collective-permute-start.1 = (bf16[2,12,128,256]{3,2,1,0:T(8,128)(2,1)}, bf16[2,12,128,256]{3,2,1,0:T(8,128)(2,1)}, u32[]{:S(2)}, u32[]{:S(2)}) collective-permute-start(bf16[2,12,128,256]{3,2,1,0:T(8,128)(2,1)} %get-tuple-element.15), channel_id=1, source_target_pairs={{1,0},{2,1},{3,2},{4,3},{5,4},{6,5},{7,6},{8,7},{9,8},{10,9},{11,1... | collective-permute-start | bytes 4718600 | tf_op jit(solution)/shard_map/ppermute | solution.py:15
  76.7 0.0 copy-done.5
  76.7 0.1 copy.37
  76.8 0.0 copy-done.10
  76.8 0.1 copy.36
  76.9 0.1 reshape.179.index_ref
  77.0 0.0 copy-start.2
  77.0 41.7 %collective-permute-done.low_ref = bf16[2,12,128,256]{3,2,1,0:T(8,128)(2,1)} collective-permute-done((bf16[2,12,128,256]{3,2,1,0:T(8,128)(2,1)}, bf16[2,12,128,256]{3,2,1,0:T(8,128)(2,1)}, u32[]{:S(2)}, u32[]{:S(2)}) %collective-permute-start) | collective-permute-done | bytes 1572896 | tf_op jit(solution)/shard_map/ppermute | solution.py:15
  118.8 2.9 %collective-permute-done.1.up_ref = bf16[2,12,128,256]{3,2,1,0:T(8,128)(2,1)} collective-permute-done((bf16[2,12,128,256]{3,2,1,0:T(8,128)(2,1)}, bf16[2,12,128,256]{3,2,1,0:T(8,128)(2,1)}, u32[]{:S(2)}, u32[]{:S(2)}) %collective-permute-start.1) | collective-permute-done | bytes 1572896 | tf_op jit(solution)/shard_map/ppermute | solution.py:15
  121.7 0.0 copy-done.6
  121.7 34.1 %near_products.1 = bf16[2,24,128,256]{3,2,1,0:T(8,128)(2,1)} custom-call(s32[216]{0:T(256)S(1)} %reshape.179.index_ref, s32[24]{0:T(128)S(1)} %copy-done.6, bf16[2,12,128,256]{3,2,1,0:T(8,128)(2,1)} %collective-permute-done.low_ref, bf16[2,24,128,256]{3,2,1,0:T(8,128)(2,1)} %cur_ref.1, bf16[2,12,128,256]{3,2,1,0:T(8,128)(2,1)} %collective-permute-done.1.up_ref, ...), custom_call_target="tpu_custom_call" | custom-call | flops 7247757312 | bytes 26738688 | tf_op jit(solution)/shard_map/near_products/pallas_call | solution.py:158
  155.8 0.0 all-to-all-done.1.in_ref
  155.8 0.0 copy-done.2
  155.8 9.9 %downward.1 = bf16[2,3,8,128,256]{4,3,2,1,0:T(8,128)(2,1)} custom-call(bf16[32,2,3,16,256]{4,3,2,1,0:T(8,128)(2,1)S(1)} %all-to-all-done.1.in_ref, bf16[2,3,8,128,256]{4,3,2,1,0:T(8,128)(2,1)} %bitcast.26, bf16[3,8,2,128,128]{4,3,2,1,0:T(8,128)(2,1)S(1)} %bitcast.22, bf16[128,512]{1,0:T(8,128)(2,1)S(1)} %bitcast.24, ...), custom_call_target="tpu_custom_call" | custom-call | tf_op jit(solution)/shard_map/downward/pallas_call | solution.py:315
  (13 shorter events, 0.1 us)
Async XLA Ops:
  1.1 1.4 copy-start.3
  2.5 0.9 copy-start.4
  15.0 6.2 %copy-start.8 = (s32[96,48]{0,1:T(8,128)S(1)}, s32[96,48]{0,1:T(8,128)}, u32[]{:S(2)}) copy-start(s32[96,48]{0,1:T(8,128)} %param.22) | copy-start | bytes 55300
  15.0 6.2 %copy-start.11 = (s32[96]{0:T(128)S(1)}, s32[96]{0:T(128)}, u32[]{:S(2)}) copy-start(s32[96]{0:T(128)} %param.21) | copy-start | bytes 1156
  15.0 6.4 %copy-start.7 = (f32[316,2,16]{0,2,1:T(8,128)S(1)}, f32[316,2,16]{0,2,1:T(8,128)}, u32[]{:S(2)}) copy-start(f32[316,2,16]{0,2,1:T(8,128)} %param.23) | copy-start | bytes 121348
  15.0 41.5 %all-to-all-start = ((bf16[32,2,3,16,256]{4,3,2,1,0:T(8,128)(2,1)}), bf16[32,2,3,16,256]{4,3,2,1,0:T(8,128)(2,1)S(1)}, u32[]{:S(2)}, u32[]{:S(2)}) async-start(bf16[32,2,3,16,256]{4,3,2,1,0:T(8,128)(2,1)} %upward.1), calls=%async_computation | async-start | bytes 3145728 | tf_op jit(solution)/shard_map/all_to_all | solution.py:360
  21.2 2.1 %copy-start.9 = (s32[96,48]{0,1:T(8,128)S(1)}, s32[96,48]{0,1:T(8,128)}, u32[]{:S(2)}) copy-start(s32[96,48]{0,1:T(8,128)} %param.20) | copy-start | bytes 55300
  32.7 1.2 copy-start
  56.5 1.4 copy-start.1
  61.4 94.3 %all-to-all-start.1 = ((bf16[32,2,3,16,256]{4,3,2,1,0:T(8,128)(2,1)}), bf16[32,2,3,16,256]{4,3,2,1,0:T(8,128)(2,1)S(1)}, u32[]{:S(2)}, u32[]{:S(2)}) async-start(bf16[32,2,3,16,256]{4,3,2,1,0:T(8,128)(2,1)} %bitcast.8), calls=%async_computation.1 | async-start | bytes 3145728 | tf_op jit(solution)/shard_map/all_to_all | solution.py:367
  67.4 9.3 %copy-start.5 = (bf16[512,128]{1,0:T(8,128)(2,1)S(1)}, bf16[512,128]{1,0:T(8,128)(2,1)}, u32[]{:S(2)}) copy-start(bf16[512,128]{1,0:T(8,128)(2,1)} %interp_ref.1) | copy-start | bytes 393220
  67.4 9.4 %copy-start.10 = (s32[24,9]{0,1:T(8,128)S(1)}, s32[24,9]{0,1:T(8,128)}, u32[]{:S(2)}) copy-start(s32[24,9]{0,1:T(8,128)} %param.14) | copy-start | bytes 2596
  67.4 54.3 %copy-start.6 = (s32[24]{0:T(128)S(1)}, s32[24]{0:T(128)}, u32[]{:S(2)}) copy-start(s32[24]{0:T(128)} %count_ref) | copy-start | bytes 292
  71.3 47.4 %collective-permute-start = (bf16[2,12,128,256]{3,2,1,0:T(8,128)(2,1)}, bf16[2,12,128,256]{3,2,1,0:T(8,128)(2,1)}, u32[]{:S(2)}, u32[]{:S(2)}) collective-permute-start(bf16[2,12,128,256]{3,2,1,0:T(8,128)(2,1)} %get-tuple-element.16), channel_id=1, source_target_pairs={{0,1},{1,2},{2,3},{3,4},{4,5},{5,6},{6,7},{7,8},{8,9},{9,10},{10,1... | collective-permute-start | bytes 4718600 | tf_op jit(solution)/shard_map/ppermute | solution.py:15
  74.7 47.0 %collective-permute-start.1 = (bf16[2,12,128,256]{3,2,1,0:T(8,128)(2,1)}, bf16[2,12,128,256]{3,2,1,0:T(8,128)(2,1)}, u32[]{:S(2)}, u32[]{:S(2)}) collective-permute-start(bf16[2,12,128,256]{3,2,1,0:T(8,128)(2,1)} %get-tuple-element.15), channel_id=1, source_target_pairs={{1,0},{2,1},{3,2},{4,3},{5,4},{6,5},{7,6},{8,7},{9,8},{10,9},{11,1... | collective-permute-start | bytes 4718600 | tf_op jit(solution)/shard_map/ppermute | solution.py:15
  77.0 78.7 %copy-start.2 = (bf16[24,2,128,128]{3,2,1,0:T(8,128)(2,1)S(1)}, bf16[24,2,128,128]{3,2,1,0:T(8,128)(2,1)}, u32[]{:S(2)}) copy-start(bf16[24,2,128,128]{3,2,1,0:T(8,128)(2,1)} %param.17) | copy-start | bytes 4718596
where the time goes:
time: 167 us; the launch traced here: 166 us
  waiting for transfers between devices  67.3 us (40%)
  Pallas kernels  66.3 us (40%)
  starting transfers between devices  17.4 us (10%)
  local copies, waits for them, and re-layouts  11.7 us (7%)
  matrix products  2.6 us (2%)
    ppermute x2, waiting for transfers between devices, passed_along(): return lax.ppermute(value, axis, pairs)  44.6 us
    pallas_call x1, Pallas kernels, near_products(): pl.pallas_call(body, grid_spec=pltpu.PrefetchScalarGridSpec(num_scalar_pr...  34.1 us
    all_to_all x1, waiting for transfers between devices, local(): lax.all_to_all(parent, AXES, split_axis=0, concat_axis=0, tiled=True)  22.6 us
    pallas_call x1, Pallas kernels, upward(): pl.pallas_call(body, grid=(12,), in_specs=[pl.BlockSpec((2, parents, 1, u...  11.6 us
    pallas_call x1, Pallas kernels, downward(): pl.pallas_call(body, grid=(8,), in_specs=[pl.BlockSpec(incoming.shape, la...  9.87 us
    pallas_call x1, Pallas kernels, wire_matrix(): pl.pallas_call(body, grid=(share,), in_specs=[pl.BlockSpec((1, total, tot...  7.17 us
    all_to_all x1, starting transfers between devices, local(): lax.all_to_all(parent, AXES, split_axis=0, concat_axis=0, tiled=True)  6.18 us
    all_to_all x1, starting transfers between devices, local(): lax.all_to_all(translated, AXES, split_axis=0, concat_axis=0, tiled=True)  5.91 us
  transfers between devices with their start and end apart: 4, of which 3 were waited for; matrix products, arithmetic and copies ran while one was open for 5% of the time, Pallas kernels for 25%

commit v1 on v0

--- a/solution.py
+++ b/solution.py
@@ -30,7 +30,6 @@
     parents = boxes // 8
     directions, leaf_dirs = interp.shape
     share = directions // parts
-    half = directions // 2
     split = share % 16 == 0
     width = 2 * leaf_dirs
     currents = currents.reshape(2, parents, 8, unknowns, columns)
@@ -45,7 +44,7 @@
             for c in range(8):
                 real = (wide * cos_ref[:, c : c + 1]).astype(jnp.bfloat16)
                 imag = (wide * sin_ref[:, c : c + 1]).astype(jnp.bfloat16)
-                shift_ref[c] = complex_matrix(real, imag)
+                shift_ref[:, c * width : (c + 1) * width] = complex_matrix(real, imag)
 
         @pl.when(step < 8)
         def _():
@@ -54,19 +53,17 @@
                 mat = complex_matrix(rad_ref[parent, 0, 0], rad_ref[parent, 0, 1])
                 vec = jnp.concatenate([cur_ref[0, parent, 0], cur_ref[1, parent, 0]], axis=0)
                 leaf = dot(mat, vec).astype(jnp.bfloat16)
-                leaf_ref[rows, parent * columns : (parent + 1) * columns] = leaf
+                leaf_ref[parent, rows, :] = leaf
         @pl.when(step >= 8)
         def _():
-            quarter = step - 8
-            rows = pl.ds(pl.multiple_of(quarter * half, half), half)
-            mat = jnp.concatenate([shift_ref[c, rows, :] for c in range(8)], axis=1)
-            result = dot(mat, leaf_ref[...]).astype(jnp.bfloat16)
-            for parent in range(parents):
-                piece = result[:, parent * columns : (parent + 1) * columns]
+            source = leaf_ref[step - 8]
+            for part in range(2):
+                rows = slice(part * directions, (part + 1) * directions)
+                piece = dot(shift_ref[rows, :], source).astype(jnp.bfloat16)
                 if split:
-                    out_ref[:, 0, parent] = piece.reshape(half // share, share, columns)
+                    out_ref[:, part, 0] = piece.reshape(parts, share, columns)
                 else:
-                    out_ref[0, parent] = piece
+                    out_ref[part, 0] = piece
 
     def early(i):
         return jnp.minimum(i, 7)
@@ -77,17 +74,16 @@
     if split:
         out_shape = (parts, 2, parents, share, columns)
         out_spec = pl.BlockSpec(
-            (parts // 2, 1, parents, share, columns),
-            lambda i: (late(i) % 2, late(i) // 2, 0, 0, 0),
+            (parts, 2, 1, share, columns), lambda i: (0, 0, late(i), 0, 0)
         )
     else:
         out_shape = (2, parents, directions, columns)
         out_spec = pl.BlockSpec(
-            (1, parents, half, columns), lambda i: (late(i) // 2, 0, late(i) % 2, 0)
+            (2, 1, directions, columns), lambda i: (0, late(i), 0, 0)
         )
     out = pl.pallas_call(
         body,
-        grid=(12,),
+        grid=(8 + parents,),
         in_specs=[
             pl.BlockSpec((2, parents, 1, unknowns, columns), lambda i: (0, 0, early(i), 0, 0)),
             pl.BlockSpec((parents, 1, 2, leaf_dirs, unknowns), lambda i: (0, early(i), 0, 0, 0)),
@@ -98,8 +94,8 @@
         out_specs=out_spec,
         out_shape=jax.ShapeDtypeStruct(out_shape, jnp.bfloat16),
         scratch_shapes=[
-            pltpu.VMEM((8 * width, parents * columns), jnp.bfloat16),
-            pltpu.VMEM((8, 2 * directions, width), jnp.bfloat16),
+            pltpu.VMEM((parents, 8 * width, columns), jnp.bfloat16),
+            pltpu.VMEM((2 * directions, 8 * width), jnp.bfloat16),
         ],
         compiler_params=pltpu.CompilerParams(vmem_limit_bytes=VMEM_BYTES),
         name="upward",
@@ -285,50 +281,55 @@
     if not split:
         incoming = jnp.transpose(incoming, (1, 2, 0, 3, 4)).reshape(2, parents, directions, columns)
 
-    def body(in_ref, near_ref, rec_ref, interp_ref, cos_ref, sin_ref, out_ref, source):
+    width = 2 * leaf_dirs
+
+    def body(in_ref, near_ref, rec_ref, interp_ref, cos_ref, sin_ref, out_ref, shift_ref, arriving):
         @pl.when(pl.program_id(0) == 0)
         def _():
+            wide = interp_ref[...].astype(jnp.float32)
+            for c in range(8):
+                real = (wide * cos_ref[c : c + 1, :]).astype(jnp.bfloat16)
+                imag = (wide * sin_ref[c : c + 1, :]).astype(jnp.bfloat16)
+                shift_ref[c * width : (c + 1) * width, :] = complex_matrix(real, -imag)
+
+        pieces = [
+            in_ref[:, part, 0].reshape(directions, columns) if split else in_ref[part, 0]
+            for part in range(2)
+        ]
+        source = jnp.concatenate(pieces, axis=0)
+        arriving[...] = dot(shift_ref[...], source).astype(jnp.bfloat16)
+        for c in range(8):
+            mat = complex_matrix(rec_ref[0, c, 0], rec_ref[0, c, 1])
+            far = dot(mat, arriving[c * width : (c + 1) * width, :])
             for part in range(2):
-                for parent in range(parents):
-                    if split:
-                        piece = in_ref[:, part, parent].reshape(directions, columns)
-                    else:
-                        piece = in_ref[part, parent]
-                    source[
-                        part * directions : (part + 1) * directions,
-                        parent * columns : (parent + 1) * columns,
-                    ] = piece
-
-        wide = interp_ref[...].astype(jnp.float32)
-        real = (wide * cos_ref[0]).astype(jnp.bfloat16)
-        imag = (wide * sin_ref[0]).astype(jnp.bfloat16)
-        arriving = dot(complex_matrix(real, -imag), source[...]).astype(jnp.bfloat16)
-        for parent in range(parents):
-            mat = complex_matrix(rec_ref[parent, 0, 0], rec_ref[parent, 0, 1])
-            far = dot(mat, arriving[:, parent * columns : (parent + 1) * columns])
-            for part in range(2):
-                total = near_ref[part, parent, 0].astype(jnp.float32)
+                total = near_ref[part, 0, c].astype(jnp.float32)
                 total = total + far[part * unknowns : (part + 1) * unknowns]
-                out_ref[part, parent, 0] = total.astype(jnp.bfloat16)
-
-    whole = (0,) * incoming.ndim
+                out_ref[part, 0, c] = total.astype(jnp.bfloat16)
+
+    if split:
+        in_spec = pl.BlockSpec((parts, 2, 1, share, columns), lambda p: (0, 0, p, 0, 0))
+    else:
+        in_spec = pl.BlockSpec((2, 1, directions, columns), lambda p: (0, p, 0, 0))
     out = pl.pallas_call(
         body,
-        grid=(8,),
+        grid=(parents,),
         in_specs=[
-            pl.BlockSpec(incoming.shape, lambda i: whole),
-            pl.BlockSpec((2, parents, 1, unknowns, columns), lambda i: (0, 0, i, 0, 0)),
-            pl.BlockSpec((parents, 1, 2, unknowns, leaf_dirs), lambda i: (0, i, 0, 0, 0)),
-            pl.BlockSpec((leaf_dirs, directions), lambda i: (0, 0)),
-            pl.BlockSpec((1, 1, directions), lambda i: (i, 0, 0)),
-            pl.BlockSpec((1, 1, directions), lambda i: (i, 0, 0)),
-        ],
-        out_specs=pl.BlockSpec((2, parents, 1, unknowns, columns), lambda i: (0, 0, i, 0, 0)),
+            in_spec,
+            pl.BlockSpec((2, 1, 8, unknowns, columns), lambda p: (0, p, 0, 0, 0)),
+            pl.BlockSpec((1, 8, 2, unknowns, leaf_dirs), lambda p: (p, 0, 0, 0, 0)),
+            pl.BlockSpec((leaf_dirs, directions), lambda p: (0, 0)),
+            pl.BlockSpec((8, directions), lambda p: (0, 0)),
+            pl.BlockSpec((8, directions), lambda p: (0, 0)),
+        ],
+        out_specs=pl.BlockSpec((2, 1, 8, unknowns, columns), lambda p: (0, p, 0, 0, 0)),
         out_shape=jax.ShapeDtypeStruct(near.shape, jnp.bfloat16),
-        scratch_shapes=[pltpu.VMEM((2 * directions, parents * columns), jnp.bfloat16)],
+        scratch_shapes=[
+            pltpu.VMEM((8 * width, 2 * directions), jnp.bfloat16),
+            pltpu.VMEM((8 * width, columns), jnp.bfloat16),
+        ],
         compiler_params=pltpu.CompilerParams(vmem_limit_bytes=VMEM_BYTES),
         name="downward",
-    )(incoming, near, receive, interp_t, cosine[:, None, :], sine[:, None, :])
+    )(incoming, near, receive, interp_t, cosine, sine)
     return out.reshape(2, boxes, unknowns, columns)
 
 
@@ -354,16 +355,18 @@
     cosine = jnp.cos(shift_angle)
     sine = jnp.sin(shift_angle)
     parent = upward(currents, radiate, interp, cosine, sine, parts)
-    parent, near_count, far_index, trans_index, translators = lax.optimization_barrier(
-        (parent, near_count, far_index, trans_index, translators)
+    parent, far_index, trans_index, translators = lax.optimization_barrier(
+        (parent, far_index, trans_index, translators)
     )
     by_direction = lax.all_to_all(parent, AXES, split_axis=0, concat_axis=0, tiled=True)
     matrix = wire_matrix(
         translation_matrix(far_index, far_count, trans_index, translators), parts
     )
     first = lax.axis_index(AXES) * boxes - reach
+    by_direction, lower, upper = lax.optimization_barrier((by_direction, lower, upper))
+    translated = translate(by_direction, matrix)
+    translated, near_count = lax.optimization_barrier((translated, near_count))
     near = near_products(lower, currents, upper, near_tiles, near_index, near_count, first)
-    translated = translate(by_direction, matrix)
     incoming = lax.all_to_all(translated, AXES, split_axis=0, concat_axis=0, tiled=True)
     return downward(incoming, near, receive, interp.T, cosine, sine)
 

time: 167 us -> 132 us (0.79)
  the two profiles are of different devices: /device:TPU:25 before, /device:TPU:0 now
where the time goes in v1:
time: 132 us; the launch traced here: 131 us
  Pallas kernels  62.1 us (47%)
  starting transfers between devices  32.9 us (25%)
  waiting for transfers between devices  21.5 us (16%)
  local copies, waits for them, and re-layouts  11.6 us (9%)
  matrix products  2.6 us (2%)
    pallas_call x1, Pallas kernels, near_products(): pl.pallas_call(body, grid_spec=pltpu.PrefetchScalarGridSpec(num_scalar_pr...  32 us
    all_to_all x1, starting transfers between devices, local(): lax.all_to_all(translated, AXES, split_axis=0, concat_axis=0, tiled=True)  20.9 us
    all_to_all x1, waiting for transfers between devices, local(): lax.all_to_all(parent, AXES, split_axis=0, concat_axis=0, tiled=True)  16.4 us
    pallas_call x1, Pallas kernels, upward(): pl.pallas_call(body, grid=(8 + parents,), in_specs=[pl.BlockSpec((2, pare...  11.5 us
    pallas_call x1, Pallas kernels, downward(): pl.pallas_call(body, grid=(parents,), in_specs=[in_spec, pl.BlockSpec((2,...  7.92 us
    all_to_all x1, starting transfers between devices, local(): lax.all_to_all(parent, AXES, split_axis=0, concat_axis=0, tiled=True)  7.3 us
    pallas_call x1, Pallas kernels, wire_matrix(): pl.pallas_call(body, grid=(share,), in_specs=[pl.BlockSpec((1, total, tot...  7.16 us
    all_to_all x1, waiting for transfers between devices, local(): lax.all_to_all(translated, AXES, split_axis=0, concat_axis=0, tiled=True)  5.17 us
  transfers between devices with their start and end apart: 4, of which 2 were waited for; matrix products, arithmetic and copies ran while one was open for 6% of the time, Pallas kernels for 30%

profile of v1, /device:TPU:0, one launch (start us, length us, event | category | flops | bytes accessed | tf_op | source)
XLA Modules:
  0.0 131.2 jit_solution(14601355678092694611)
XLA Ops:
  0.0 0.8 fusion.18
  0.8 0.1 copy.29.cos_ref
  0.9 0.1 copy.30.sin_ref
  1.1 0.0 copy-start.3
  1.1 1.4 %copy-done.3 = bf16[24,2,128,128]{3,2,1,0:T(8,128)(2,1)S(1)} copy-done((bf16[24,2,128,128]{3,2,1,0:T(8,128)(2,1)S(1)}, bf16[24,2,128,128]{3,2,1,0:T(8,128)(2,1)}, u32[]{:S(2)}) %copy-start.3) | copy-done | bytes 1572888
  2.5 0.0 copy-start.4
  2.5 0.9 copy-done.4
  3.4 11.5 %upward.1 = bf16[32,2,3,16,256]{4,3,2,1,0:T(8,128)(2,1)} custom-call(bf16[2,3,8,128,256]{4,3,2,1,0:T(8,128)(2,1)} %bitcast.27, bf16[3,8,2,128,128]{4,3,2,1,0:T(8,128)(2,1)S(1)} %bitcast.23, bf16[512,128]{1,0:T(8,128)(2,1)S(1)} %copy-done.4, f32[512,8]{1,0:T(8,128)S(1)} %copy.29.cos_ref, f32[512,8]{1,0:T(8,128)S(1)} %copy.30.sin_ref), custom_call_target="tpu_custom_call" | custom-call | tf_op jit(solution)/shard_map/upward/pallas_call | solution.py:84
  14.9 7.3 %all-to-all-start = ((bf16[32,2,3,16,256]{4,3,2,1,0:T(8,128)(2,1)}), bf16[32,2,3,16,256]{4,3,2,1,0:T(8,128)(2,1)S(1)}, u32[]{:S(2)}, u32[]{:S(2)}) async-start(bf16[32,2,3,16,256]{4,3,2,1,0:T(8,128)(2,1)} %upward.1), calls=%async_computation | async-start | bytes 3145728 | tf_op jit(solution)/shard_map/all_to_all | solution.py:361
  22.2 0.0 copy-start.8
  22.2 0.0 copy-start.11
  22.2 0.0 copy-start.7
  22.2 3.9 %fusion.17 = (bf16[2,12,128,256]{3,2,1,0:T(8,128)(2,1)}, bf16[2,12,128,256]{3,2,1,0:T(8,128)(2,1)}) fusion(bf16[2,24,128,256]{3,2,1,0:T(8,128)(2,1)} %cur_ref.1), kind=kLoop, calls=%fused_computation.36 | loop fusion | bytes 6291456 | tf_op jit(solution)/shard_map/slice | solution.py:354
  26.1 0.0 copy-start.9
  26.1 3.4 %collective-permute-start = (bf16[2,12,128,256]{3,2,1,0:T(8,128)(2,1)}, bf16[2,12,128,256]{3,2,1,0:T(8,128)(2,1)}, u32[]{:S(2)}, u32[]{:S(2)}) collective-permute-start(bf16[2,12,128,256]{3,2,1,0:T(8,128)(2,1)} %get-tuple-element.24), channel_id=1, source_target_pairs={{0,1},{1,2},{2,3},{3,4},{4,5},{5,6},{6,7},{7,8},{8,9},{9,10},{10,1... | collective-permute-start | bytes 4718600 | tf_op jit(solution)/shard_map/ppermute | solution.py:15
  29.6 1.3 collective-permute-start.1
  30.9 0.0 copy-done.8
  30.9 0.0 copy-done.11
  30.9 0.1 copy.32
  31.0 0.1 eq.80
  31.1 0.0 copy-done.7
  31.1 1.1 fusion.1
  32.2 0.8 reshape.177
  33.0 0.0 copy-done.9
  33.0 0.1 copy.31
  33.1 1.5 %fusion.3 = bf16[96,96,32]{1,2,0:T(8,128)(2,1)S(1)} fusion(s32[96,48]{1,0:T(8,128)S(1)} %copy.31, bf16[96,48,32]{1,0,2:T(8,128)(2,1)S(1)} %reshape.177), kind=kOutput, calls=%fused_computation.5 | convolution fusion | flops 28753920 | bytes 903168 | tf_op jit(solution)/shard_map/psx,psq->xpq/dot_general | solution.py:199
  34.6 0.3 copy.43
  35.1 0.1 copy.35.spread_ref
  35.2 7.2 %wire_matrix.1.mat_ref = bf16[16,192,192]{2,1,0:T(8,128)(2,1)S(1)} custom-call(bf16[32,96,96]{2,1,0:T(8,128)(2,1)S(1)} %bitcast.19, bf16[32,96,96]{2,1,0:T(8,128)(2,1)S(1)} %bitcast.20, bf16[2,192,96]{2,1,0:T(8,128)(2,1)S(1)} %copy.35.spread_ref, bf16[2,96,192]{2,1,0:T(8,128)(2,1)S(1)} %get-tuple-element.25.gather_ref), custom_call_target="tpu_custom_call" | custom-call | flops 226492416 | bytes 1769472 | tf_op jit(solution)/shard_map/wire_matrix/pallas_call | solution.py:223
  42.3 0.0 copy-start
  42.4 1.2 copy-done
  43.5 0.0 collective-permute-done.low_ref
  43.5 0.0 collective-permute-done.1.up_ref
  43.5 16.4 %all-to-all-done = bf16[32,2,3,16,256]{4,3,2,1,0:T(8,128)(2,1)S(1)} async-done(((bf16[32,2,3,16,256]{4,3,2,1,0:T(8,128)(2,1)}), bf16[32,2,3,16,256]{4,3,2,1,0:T(8,128)(2,1)S(1)}, u32[]{:S(2)}, u32[]{:S(2)}) %all-to-all-start) | async-done | bytes 1572896 | tf_op jit(solution)/shard_map/all_to_all | solution.py:361
  59.9 1.4 %copy-done.1 = bf16[16,192,192]{2,1,0:T(8,128)(2,1)S(1)} copy-done((bf16[16,192,192]{2,1,0:T(8,128)(2,1)S(1)}, bf16[16,192,192]{2,1,0:T(8,128)(2,1)}, u32[]{:S(2)}) %copy-start.1) | copy-done | bytes 1179672
  61.3 3.5 %translate.1 = bf16[3072,256]{1,0:T(8,128)(2,1)} custom-call(bf16[3072,256]{1,0:T(8,128)(2,1)S(1)} %bitcast.21, bf16[16,192,192]{2,1,0:T(8,128)(2,1)S(1)} %copy-done.1), custom_call_target="tpu_custom_call" | custom-call | tf_op jit(solution)/shard_map/translate/pallas_call | solution.py:255
  64.8 20.9 %all-to-all-start.1 = ((bf16[32,2,3,16,256]{4,3,2,1,0:T(8,128)(2,1)}), bf16[32,2,3,16,256]{4,3,2,1,0:T(8,128)(2,1)S(1)}, u32[]{:S(2)}, u32[]{:S(2)}) async-start(bf16[32,2,3,16,256]{4,3,2,1,0:T(8,128)(2,1)} %bitcast.8), calls=%async_computation.1 | async-start | bytes 3145728 | tf_op jit(solution)/shard_map/all_to_all | solution.py:370
  85.8 0.0 copy-done.5
  85.8 0.1 copy.37
  85.9 0.0 copy-done.10
  85.9 0.1 copy.36
  86.0 0.1 reshape.179.index_ref
  86.1 0.0 copy-done.6
  86.1 0.0 copy-start.2
  86.1 32.0 %near_products.1 = bf16[2,24,128,256]{3,2,1,0:T(8,128)(2,1)} custom-call(s32[216]{0:T(256)S(1)} %reshape.179.index_ref, s32[24]{0:T(128)S(1)} %copy-done.6, bf16[2,12,128,256]{3,2,1,0:T(8,128)(2,1)} %collective-permute-done.low_ref, bf16[2,24,128,256]{3,2,1,0:T(8,128)(2,1)} %cur_ref.1, bf16[2,12,128,256]{3,2,1,0:T(8,128)(2,1)} %collective-permute-done.1.up_ref, ...), custom_call_target="tpu_custom_call" | custom-call | flops 7247757312 | bytes 26738688 | tf_op jit(solution)/shard_map/near_products/pallas_call | solution.py:154
  118.1 5.2 %all-to-all-done.1.in_ref = bf16[32,2,3,16,256]{4,3,2,1,0:T(8,128)(2,1)S(1)} async-done(((bf16[32,2,3,16,256]{4,3,2,1,0:T(8,128)(2,1)}), bf16[32,2,3,16,256]{4,3,2,1,0:T(8,128)(2,1)S(1)}, u32[]{:S(2)}, u32[]{:S(2)}) %all-to-all-start.1) | async-done | bytes 1572896 | tf_op jit(solution)/shard_map/all_to_all | solution.py:370
  123.3 0.0 copy-done.2
  123.3 7.9 %downward.1 = bf16[2,3,8,128,256]{4,3,2,1,0:T(8,128)(2,1)} custom-call(bf16[32,2,3,16,256]{4,3,2,1,0:T(8,128)(2,1)S(1)} %all-to-all-done.1.in_ref, bf16[2,3,8,128,256]{4,3,2,1,0:T(8,128)(2,1)} %bitcast.28, bf16[3,8,2,128,128]{4,3,2,1,0:T(8,128)(2,1)S(1)} %bitcast.22, bf16[128,512]{1,0:T(8,128)(2,1)S(1)} %bitcast.24, f32[8,512]{1,0:T(8,128)S(1)} %get-tuple-element.28.cos_ref, ...), custom_call_target="tpu_custom_call" | custom-call | tf_op jit(solution)/shard_map/downward/pallas_call | solution.py:313
  (11 shorter events, 0.1 us)
Async XLA Ops:
  1.1 1.4 %copy-start.3 = (bf16[24,2,128,128]{3,2,1,0:T(8,128)(2,1)S(1)}, bf16[24,2,128,128]{3,2,1,0:T(8,128)(2,1)}, u32[]{:S(2)}) copy-start(bf16[24,2,128,128]{3,2,1,0:T(8,128)(2,1)} %param.16) | copy-start | bytes 4718596
  2.5 0.9 copy-start.4
  14.9 45.0 %all-to-all-start = ((bf16[32,2,3,16,256]{4,3,2,1,0:T(8,128)(2,1)}), bf16[32,2,3,16,256]{4,3,2,1,0:T(8,128)(2,1)S(1)}, u32[]{:S(2)}, u32[]{:S(2)}) async-start(bf16[32,2,3,16,256]{4,3,2,1,0:T(8,128)(2,1)} %upward.1), calls=%async_computation | async-start | bytes 3145728 | tf_op jit(solution)/shard_map/all_to_all | solution.py:361
  22.2 8.7 %copy-start.8 = (s32[96,48]{0,1:T(8,128)S(1)}, s32[96,48]{0,1:T(8,128)}, u32[]{:S(2)}) copy-start(s32[96,48]{0,1:T(8,128)} %param.22) | copy-start | bytes 55300
  22.2 8.7 %copy-start.11 = (s32[96]{0:T(128)S(1)}, s32[96]{0:T(128)}, u32[]{:S(2)}) copy-start(s32[96]{0:T(128)} %param.21) | copy-start | bytes 1156
  22.2 8.9 %copy-start.7 = (f32[316,2,16]{0,2,1:T(8,128)S(1)}, f32[316,2,16]{0,2,1:T(8,128)}, u32[]{:S(2)}) copy-start(f32[316,2,16]{0,2,1:T(8,128)} %param.23) | copy-start | bytes 121348
  26.1 6.9 %copy-start.9 = (s32[96,48]{0,1:T(8,128)S(1)}, s32[96,48]{0,1:T(8,128)}, u32[]{:S(2)}) copy-start(s32[96,48]{0,1:T(8,128)} %param.20) | copy-start | bytes 55300
  26.1 17.4 %collective-permute-start = (bf16[2,12,128,256]{3,2,1,0:T(8,128)(2,1)}, bf16[2,12,128,256]{3,2,1,0:T(8,128)(2,1)}, u32[]{:S(2)}, u32[]{:S(2)}) collective-permute-start(bf16[2,12,128,256]{3,2,1,0:T(8,128)(2,1)} %get-tuple-element.24), channel_id=1, source_target_pairs={{0,1},{1,2},{2,3},{3,4},{4,5},{5,6},{6,7},{7,8},{8,9},{9,10},{10,1... | collective-permute-start | bytes 4718600 | tf_op jit(solution)/shard_map/ppermute | solution.py:15
  29.6 13.9 %collective-permute-start.1 = (bf16[2,12,128,256]{3,2,1,0:T(8,128)(2,1)}, bf16[2,12,128,256]{3,2,1,0:T(8,128)(2,1)}, u32[]{:S(2)}, u32[]{:S(2)}) collective-permute-start(bf16[2,12,128,256]{3,2,1,0:T(8,128)(2,1)} %get-tuple-element.23), channel_id=1, source_target_pairs={{1,0},{2,1},{3,2},{4,3},{5,4},{6,5},{7,6},{8,7},{9,8},{10,9},{11,1... | collective-permute-start | bytes 4718600 | tf_op jit(solution)/shard_map/ppermute | solution.py:15
  42.3 1.2 copy-start
  59.9 1.4 %copy-start.1 = (bf16[16,192,192]{2,1,0:T(8,128)(2,1)S(1)}, bf16[16,192,192]{2,1,0:T(8,128)(2,1)}, u32[]{:S(2)}) copy-start(bf16[16,192,192]{2,1,0:T(8,128)(2,1)} %copy-done) | copy-start | bytes 3538948
  64.8 20.9 %copy-start.5 = (bf16[512,128]{1,0:T(8,128)(2,1)S(1)}, bf16[512,128]{1,0:T(8,128)(2,1)}, u32[]{:S(2)}) copy-start(bf16[512,128]{1,0:T(8,128)(2,1)} %interp_ref.1) | copy-start | bytes 393220
  64.8 21.1 %copy-start.10 = (s32[24,9]{0,1:T(8,128)S(1)}, s32[24,9]{0,1:T(8,128)}, u32[]{:S(2)}) copy-start(s32[24,9]{0,1:T(8,128)} %param.14) | copy-start | bytes 2596
  64.8 21.3 %copy-start.6 = (s32[24]{0:T(128)S(1)}, s32[24]{0:T(128)}, u32[]{:S(2)}) copy-start(s32[24]{0:T(128)} %count_ref) | copy-start | bytes 292
  64.8 58.4 %all-to-all-start.1 = ((bf16[32,2,3,16,256]{4,3,2,1,0:T(8,128)(2,1)}), bf16[32,2,3,16,256]{4,3,2,1,0:T(8,128)(2,1)S(1)}, u32[]{:S(2)}, u32[]{:S(2)}) async-start(bf16[32,2,3,16,256]{4,3,2,1,0:T(8,128)(2,1)} %bitcast.8), calls=%async_computation.1 | async-start | bytes 3145728 | tf_op jit(solution)/shard_map/all_to_all | solution.py:370
  86.1 37.2 %copy-start.2 = (bf16[24,2,128,128]{3,2,1,0:T(8,128)(2,1)S(1)}, bf16[24,2,128,128]{3,2,1,0:T(8,128)(2,1)}, u32[]{:S(2)}) copy-start(bf16[24,2,128,128]{3,2,1,0:T(8,128)(2,1)} %param.17) | copy-start | bytes 4718596

commit v2 on v1

--- a/solution.py
+++ b/solution.py
@@ -98,6 +98,11 @@
             pltpu.VMEM((2 * directions, 8 * width), jnp.bfloat16),
         ],
         compiler_params=pltpu.CompilerParams(vmem_limit_bytes=VMEM_BYTES),
+        cost_estimate=pl.CostEstimate(
+            flops=8 * boxes * leaf_dirs * columns * (unknowns + directions),
+            bytes_accessed=2 * (currents.size + radiate.size + 2 * parents * directions * columns),
+            transcendentals=0,
+        ),
         name="upward",
     )(currents, radiate, interp, cosine.T, sine.T)
     if not split:
@@ -355,15 +360,14 @@
     cosine = jnp.cos(shift_angle)
     sine = jnp.sin(shift_angle)
     parent = upward(currents, radiate, interp, cosine, sine, parts)
-    parent, far_index, trans_index, translators = lax.optimization_barrier(
-        (parent, far_index, trans_index, translators)
+    parent, lower, upper, far_index, trans_index, translators = lax.optimization_barrier(
+        (parent, lower, upper, far_index, trans_index, translators)
     )
     by_direction = lax.all_to_all(parent, AXES, split_axis=0, concat_axis=0, tiled=True)
     matrix = wire_matrix(
         translation_matrix(far_index, far_count, trans_index, translators), parts
     )
     first = lax.axis_index(AXES) * boxes - reach
-    by_direction, lower, upper = lax.optimization_barrier((by_direction, lower, upper))
     translated = translate(by_direction, matrix)
     translated, near_count = lax.optimization_barrier((translated, near_count))
     near = near_products(lower, currents, upper, near_tiles, near_index, near_count, first)

time: 132 us -> 141 us (1.068)
  waiting for transfers between devices: 21.5 us -> 27.6 us
  local copies, waits for them, and re-layouts: 11.6 us -> 6.15 us
  starting transfers between devices: 32.9 us -> 37.3 us
  Pallas kernels: 62.1 us -> 65.7 us
    all_to_all x1, starting transfers between devices: 7.3 us -> 28.8 us  [local(): lax.all_to_all(parent, AXES, split_axis=0, concat_axis=0, tiled=True)]
    all_to_all x1, starting transfers between devices: 20.9 us -> 3.66 us  [local(): lax.all_to_all(translated, AXES, split_axis=0, concat_axis=0, tiled=True)]
    all_to_all x1, waiting for transfers between devices: 16.4 us -> 26 us  [local(): lax.all_to_all(parent, AXES, split_axis=0, concat_axis=0, tiled=True)]
    unnamed x25 -> x21, local copies, waits for them, and re-layouts: 5.02 us -> 0.16 us
    pallas_call x1, Pallas kernels: 32 us -> 35.6 us  [near_products(): pl.pallas_call(body, grid_spec=pltpu.PrefetchScalarGridSpec(num_scalar_pr...]
    all_to_all x1, waiting for transfers between devices: 5.17 us -> 1.6 us  [local(): lax.all_to_all(translated, AXES, split_axis=0, concat_axis=0, tiled=True)]
  transfers between devices with their start and end apart: 4 -> 4, of which waited for: 2 -> 2; matrix products, arithmetic and copies ran while one was open for 6% -> 3% of each run, Pallas kernels for 30% -> 39%
where the time goes in v2:
time: 141 us; the launch traced here: 140 us
  Pallas kernels  65.7 us (47%)
  starting transfers between devices  37.3 us (26%)
  waiting for transfers between devices  27.6 us (20%)
  local copies, waits for them, and re-layouts  6.15 us (4%)
  matrix products  2.6 us (2%)
    pallas_call x1, Pallas kernels, near_products(): pl.pallas_call(body, grid_spec=pltpu.PrefetchScalarGridSpec(num_scalar_pr...  35.6 us
    all_to_all x1, starting transfers between devices, local(): lax.all_to_all(parent, AXES, split_axis=0, concat_axis=0, tiled=True)  28.8 us
    all_to_all x1, waiting for transfers between devices, local(): lax.all_to_all(parent, AXES, split_axis=0, concat_axis=0, tiled=True)  26 us
    pallas_call x1, Pallas kernels, upward(): pl.pallas_call(body, grid=(8 + parents,), in_specs=[pl.BlockSpec((2, pare...  11.5 us
    pallas_call x1, Pallas kernels, downward(): pl.pallas_call(body, grid=(parents,), in_specs=[in_spec, pl.BlockSpec((2,...  7.88 us
    pallas_call x1, Pallas kernels, wire_matrix(): pl.pallas_call(body, grid=(share,), in_specs=[pl.BlockSpec((1, total, tot...  7.17 us
    ppermute x2, starting transfers between devices, passed_along(): return lax.ppermute(value, axis, pairs)  4.8 us
    slice x1, local copies, waits for them, and re-layouts, local(): upper = passed_along(currents[:, :reach], AXES, -1)  4.02 us
  transfers between devices with their start and end apart: 4, of which 2 were waited for; matrix products, arithmetic and copies ran while one was open for 3% of the time, Pallas kernels for 39%

profile of v2, /device:TPU:0, one launch (start us, length us, event | category | flops | bytes accessed | tf_op | source)
XLA Modules:
  0.0 139.7 jit_solution(9305307406916294010)
XLA Ops:
  0.0 0.0 copy-start.7
  0.0 0.0 copy-start.2
  0.0 0.0 copy-start.1
  0.0 4.0 %fusion.17 = (bf16[2,12,128,256]{3,2,1,0:T(8,128)(2,1)}, bf16[2,12,128,256]{3,2,1,0:T(8,128)(2,1)}) fusion(bf16[2,24,128,256]{3,2,1,0:T(8,128)(2,1)} %cur_ref.1), kind=kLoop, calls=%fused_computation.36 | loop fusion | bytes 6291456 | tf_op jit(solution)/shard_map/slice | solution.py:359
  4.0 3.5 %collective-permute-start = (bf16[2,12,128,256]{3,2,1,0:T(8,128)(2,1)}, bf16[2,12,128,256]{3,2,1,0:T(8,128)(2,1)}, u32[]{:S(2)}, u32[]{:S(2)}) collective-permute-start(bf16[2,12,128,256]{3,2,1,0:T(8,128)(2,1)} %get-tuple-element.22), channel_id=1, source_target_pairs={{0,1},{1,2},{2,3},{3,4},{4,5},{5,6},{6,7},{7,8},{8,9},{9,10},{10,1... | collective-permute-start | bytes 4718600 | tf_op jit(solution)/shard_map/ppermute | solution.py:15
  7.5 1.3 collective-permute-start.1
  8.8 0.0 copy-done.7
  8.8 0.1 fusion.18
  8.9 0.1 copy.29.cos_ref
  9.1 0.1 copy.30.sin_ref
  9.2 0.0 copy-done.2
  9.2 0.0 copy-done.1
  9.2 11.5 %upward.1 = bf16[32,2,3,16,256]{4,3,2,1,0:T(8,128)(2,1)} custom-call(bf16[2,3,8,128,256]{4,3,2,1,0:T(8,128)(2,1)} %bitcast.27, bf16[3,8,2,128,128]{4,3,2,1,0:T(8,128)(2,1)S(1)} %bitcast.26, bf16[512,128]{1,0:T(8,128)(2,1)S(1)} %copy-done.1, f32[512,8]{1,0:T(8,128)S(1)} %copy.29.cos_ref, f32[512,8]{1,0:T(8,128)S(1)} %copy.30.sin_ref), custom_call_target="tpu_custom_call" | custom-call | flops 4026531840 | bytes 6291456 | tf_op jit(solution)/shard_map/upward/pallas_call | solution.py:84
  20.7 0.0 copy-start.5
  20.7 0.0 copy-start.9
  20.7 0.0 copy-start.4
  20.7 0.0 collective-permute-done.low_ref
  20.8 0.0 collective-permute-done.1.up_ref
  20.8 28.8 %all-to-all-start = ((bf16[32,2,3,16,256]{4,3,2,1,0:T(8,128)(2,1)}), bf16[32,2,3,16,256]{4,3,2,1,0:T(8,128)(2,1)S(1)}, u32[]{:S(2)}, u32[]{:S(2)}) async-start(bf16[32,2,3,16,256]{4,3,2,1,0:T(8,128)(2,1)} %upward.1), calls=%async_computation | async-start | bytes 3145728 | tf_op jit(solution)/shard_map/all_to_all | solution.py:366
  49.7 0.1 copy.35.spread_ref
  49.8 0.0 copy-done.5
  49.8 0.0 copy-done.9
  49.9 0.0 copy-start.6
  49.9 0.1 copy.32
  50.0 0.1 eq.80
  50.1 0.0 copy-done.4
  50.1 1.1 fusion.1
  51.2 0.8 reshape.177
  52.0 0.0 copy-done.6
  52.0 0.1 copy.31
  52.1 1.5 %fusion.3 = bf16[96,96,32]{1,2,0:T(8,128)(2,1)S(1)} fusion(s32[96,48]{1,0:T(8,128)S(1)} %copy.31, bf16[96,48,32]{1,0,2:T(8,128)(2,1)S(1)} %reshape.177), kind=kOutput, calls=%fused_computation.5 | convolution fusion | flops 28753920 | bytes 903168 | tf_op jit(solution)/shard_map/psx,psq->xpq/dot_general | solution.py:204
  53.6 0.3 copy.43
  53.9 7.2 %wire_matrix.1.mat_ref = bf16[16,192,192]{2,1,0:T(8,128)(2,1)S(1)} custom-call(bf16[32,96,96]{2,1,0:T(8,128)(2,1)S(1)} %bitcast.19, bf16[32,96,96]{2,1,0:T(8,128)(2,1)S(1)} %bitcast.20, bf16[2,192,96]{2,1,0:T(8,128)(2,1)S(1)} %copy.35.spread_ref, bf16[2,96,192]{2,1,0:T(8,128)(2,1)S(1)} %get-tuple-element.23.gather_ref), custom_call_target="tpu_custom_call" | custom-call | flops 226492416 | bytes 1769472 | tf_op jit(solution)/shard_map/wire_matrix/pallas_call | solution.py:228
  61.1 26.0 %all-to-all-done = bf16[32,2,3,16,256]{4,3,2,1,0:T(8,128)(2,1)S(1)} async-done(((bf16[32,2,3,16,256]{4,3,2,1,0:T(8,128)(2,1)}), bf16[32,2,3,16,256]{4,3,2,1,0:T(8,128)(2,1)S(1)}, u32[]{:S(2)}, u32[]{:S(2)}) %all-to-all-start) | async-done | bytes 1572896 | tf_op jit(solution)/shard_map/all_to_all | solution.py:366
  87.1 3.5 %translate.1 = bf16[3072,256]{1,0:T(8,128)(2,1)} custom-call(bf16[3072,256]{1,0:T(8,128)(2,1)S(1)} %bitcast.21, bf16[16,192,192]{2,1,0:T(8,128)(2,1)S(1)} %wire_matrix.1.mat_ref), custom_call_target="tpu_custom_call" | custom-call | tf_op jit(solution)/shard_map/translate/pallas_call | solution.py:260
  90.7 0.0 copy-start.8
  90.7 0.0 copy-start.3
  90.7 3.7 %all-to-all-start.1 = ((bf16[32,2,3,16,256]{4,3,2,1,0:T(8,128)(2,1)}), bf16[32,2,3,16,256]{4,3,2,1,0:T(8,128)(2,1)S(1)}, u32[]{:S(2)}, u32[]{:S(2)}) async-start(bf16[32,2,3,16,256]{4,3,2,1,0:T(8,128)(2,1)} %bitcast.8), calls=%async_computation.1 | async-start | bytes 3145728 | tf_op jit(solution)/shard_map/all_to_all | solution.py:374
  94.3 0.1 copy.37
  94.5 0.0 copy-done.8
  94.5 0.1 copy.36
  94.6 0.1 reshape.179.index_ref
  94.7 0.0 copy-done.3
  94.7 0.0 copy-start
  94.7 35.6 %near_products.1 = bf16[2,24,128,256]{3,2,1,0:T(8,128)(2,1)} custom-call(s32[216]{0:T(256)S(1)} %reshape.179.index_ref, s32[24]{0:T(128)S(1)} %copy-done.3, bf16[2,12,128,256]{3,2,1,0:T(8,128)(2,1)} %collective-permute-done.low_ref, bf16[2,24,128,256]{3,2,1,0:T(8,128)(2,1)} %cur_ref.1, bf16[2,12,128,256]{3,2,1,0:T(8,128)(2,1)} %collective-permute-done.1.up_ref, ...), custom_call_target="tpu_custom_call" | custom-call | flops 7247757312 | bytes 26738688 | tf_op jit(solution)/shard_map/near_products/pallas_call | solution.py:159
  130.3 1.6 %all-to-all-done.1.in_ref = bf16[32,2,3,16,256]{4,3,2,1,0:T(8,128)(2,1)S(1)} async-done(((bf16[32,2,3,16,256]{4,3,2,1,0:T(8,128)(2,1)}), bf16[32,2,3,16,256]{4,3,2,1,0:T(8,128)(2,1)S(1)}, u32[]{:S(2)}, u32[]{:S(2)}) %all-to-all-start.1) | async-done | bytes 1572896 | tf_op jit(solution)/shard_map/all_to_all | solution.py:374
  131.9 0.0 copy-done
  131.9 7.9 %downward.1 = bf16[2,3,8,128,256]{4,3,2,1,0:T(8,128)(2,1)} custom-call(bf16[32,2,3,16,256]{4,3,2,1,0:T(8,128)(2,1)S(1)} %all-to-all-done.1.in_ref, bf16[2,3,8,128,256]{4,3,2,1,0:T(8,128)(2,1)} %bitcast.28, bf16[3,8,2,128,128]{4,3,2,1,0:T(8,128)(2,1)S(1)} %bitcast.22, bf16[128,512]{1,0:T(8,128)(2,1)S(1)} %bitcast.23, f32[8,512]{1,0:T(8,128)S(1)} %get-tuple-element.26.cos_ref, ...), custom_call_target="tpu_custom_call" | custom-call | tf_op jit(solution)/shard_map/downward/pallas_call | solution.py:318
  (7 shorter events, 0.1 us)
Async XLA Ops:
  0.0 8.8 %copy-start.7 = (f32[8,512]{1,0:T(8,128)S(1)}, f32[8,512]{1,0:T(8,128)}, u32[]{:S(2)}) copy-start(f32[8,512]{1,0:T(8,128)} %param.19) | copy-start | bytes 49156
  0.0 9.2 %copy-start.2 = (bf16[24,2,128,128]{3,2,1,0:T(8,128)(2,1)S(1)}, bf16[24,2,128,128]{3,2,1,0:T(8,128)(2,1)}, u32[]{:S(2)}) copy-start(bf16[24,2,128,128]{3,2,1,0:T(8,128)(2,1)} %param.16) | copy-start | bytes 4718596
  0.0 9.2 %copy-start.1 = (bf16[512,128]{1,0:T(8,128)(2,1)S(1)}, bf16[512,128]{1,0:T(8,128)(2,1)}, u32[]{:S(2)}) copy-start(bf16[512,128]{1,0:T(8,128)(2,1)} %interp_ref.1) | copy-start | bytes 393220
  4.0 16.7 %collective-permute-start = (bf16[2,12,128,256]{3,2,1,0:T(8,128)(2,1)}, bf16[2,12,128,256]{3,2,1,0:T(8,128)(2,1)}, u32[]{:S(2)}, u32[]{:S(2)}) collective-permute-start(bf16[2,12,128,256]{3,2,1,0:T(8,128)(2,1)} %get-tuple-element.22), channel_id=1, source_target_pairs={{0,1},{1,2},{2,3},{3,4},{4,5},{5,6},{6,7},{7,8},{8,9},{9,10},{10,1... | collective-permute-start | bytes 4718600 | tf_op jit(solution)/shard_map/ppermute | solution.py:15
  7.5 13.2 %collective-permute-start.1 = (bf16[2,12,128,256]{3,2,1,0:T(8,128)(2,1)}, bf16[2,12,128,256]{3,2,1,0:T(8,128)(2,1)}, u32[]{:S(2)}, u32[]{:S(2)}) collective-permute-start(bf16[2,12,128,256]{3,2,1,0:T(8,128)(2,1)} %get-tuple-element.21), channel_id=1, source_target_pairs={{1,0},{2,1},{3,2},{4,3},{5,4},{6,5},{7,6},{8,7},{9,8},{10,9},{11,1... | collective-permute-start | bytes 4718600 | tf_op jit(solution)/shard_map/ppermute | solution.py:15
  20.7 29.1 %copy-start.5 = (s32[96,48]{0,1:T(8,128)S(1)}, s32[96,48]{0,1:T(8,128)}, u32[]{:S(2)}) copy-start(s32[96,48]{0,1:T(8,128)} %param.22) | copy-start | bytes 55300
  20.7 29.1 %copy-start.9 = (s32[96]{0:T(128)S(1)}, s32[96]{0:T(128)}, u32[]{:S(2)}) copy-start(s32[96]{0:T(128)} %param.21) | copy-start | bytes 1156
  20.7 29.3 %copy-start.4 = (f32[316,2,16]{0,2,1:T(8,128)S(1)}, f32[316,2,16]{0,2,1:T(8,128)}, u32[]{:S(2)}) copy-start(f32[316,2,16]{0,2,1:T(8,128)} %param.23) | copy-start | bytes 121348
  20.8 66.4 %all-to-all-start = ((bf16[32,2,3,16,256]{4,3,2,1,0:T(8,128)(2,1)}), bf16[32,2,3,16,256]{4,3,2,1,0:T(8,128)(2,1)S(1)}, u32[]{:S(2)}, u32[]{:S(2)}) async-start(bf16[32,2,3,16,256]{4,3,2,1,0:T(8,128)(2,1)} %upward.1), calls=%async_computation | async-start | bytes 3145728 | tf_op jit(solution)/shard_map/all_to_all | solution.py:366
  49.9 2.1 %copy-start.6 = (s32[96,48]{0,1:T(8,128)S(1)}, s32[96,48]{0,1:T(8,128)}, u32[]{:S(2)}) copy-start(s32[96,48]{0,1:T(8,128)} %param.20) | copy-start | bytes 55300
  90.7 3.8 %copy-start.8 = (s32[24,9]{0,1:T(8,128)S(1)}, s32[24,9]{0,1:T(8,128)}, u32[]{:S(2)}) copy-start(s32[24,9]{0,1:T(8,128)} %param.14) | copy-start | bytes 2596
  90.7 4.0 %copy-start.3 = (s32[24]{0:T(128)S(1)}, s32[24]{0:T(128)}, u32[]{:S(2)}) copy-start(s32[24]{0:T(128)} %count_ref) | copy-start | bytes 292
  90.7 41.2 %all-to-all-start.1 = ((bf16[32,2,3,16,256]{4,3,2,1,0:T(8,128)(2,1)}), bf16[32,2,3,16,256]{4,3,2,1,0:T(8,128)(2,1)S(1)}, u32[]{:S(2)}, u32[]{:S(2)}) async-start(bf16[32,2,3,16,256]{4,3,2,1,0:T(8,128)(2,1)} %bitcast.8), calls=%async_computation.1 | async-start | bytes 3145728 | tf_op jit(solution)/shard_map/all_to_all | solution.py:374
  94.7 37.2 %copy-start = (bf16[24,2,128,128]{3,2,1,0:T(8,128)(2,1)S(1)}, bf16[24,2,128,128]{3,2,1,0:T(8,128)(2,1)}, u32[]{:S(2)}) copy-start(bf16[24,2,128,128]{3,2,1,0:T(8,128)(2,1)} %param.17) | copy-start | bytes 4718596

commit v3 on v2

--- a/solution.py
+++ b/solution.py
@@ -116,7 +116,20 @@
     reach = boxes // 2
     slots = near_tiles.shape[1]
 
-    def body(index_ref, count_ref, low_ref, cur_ref, up_ref, tile_ref, out_ref, window, acc, sems):
+    def body(
+        index_ref,
+        count_ref,
+        low_real,
+        low_imag,
+        cur_ref,
+        up_real,
+        up_imag,
+        tile_ref,
+        out_ref,
+        window,
+        acc,
+        sems,
+    ):
         box = pl.program_id(0)
 
         @pl.when(box == 0)
@@ -125,11 +138,15 @@
             for part in range(2):
                 rows = pl.ds(part * unknowns, unknowns)
                 for order, (ref, start, size) in enumerate(
-                    ((low_ref, 0, reach), (cur_ref, reach, boxes), (up_ref, reach + boxes, reach))
+                    (
+                        ((low_real, low_imag)[part], 0, reach),
+                        (cur_ref.at[part], reach, boxes),
+                        ((up_real, up_imag)[part], reach + boxes, reach),
+                    )
                 ):
                     copies.append(
                         pltpu.make_async_copy(
-                            ref.at[part],
+                            ref,
                             window.at[pl.ds(start, size), rows],
                             sems.at[3 * part + order],
                         )
@@ -162,6 +179,8 @@
             num_scalar_prefetch=2,
             grid=(boxes,),
             in_specs=[
+                pl.BlockSpec(memory_space=pl.ANY),
+                pl.BlockSpec(memory_space=pl.ANY),
                 pl.BlockSpec(memory_space=pl.ANY),
                 pl.BlockSpec(memory_space=pl.ANY),
                 pl.BlockSpec(memory_space=pl.ANY),
@@ -186,7 +205,7 @@
             transcendentals=0,
         ),
         name="near_products",
-    )(local_index, near_count, lower, currents, upper, near_tiles)
+    )(local_index, near_count, *lower, currents, *upper, near_tiles)
 
 
 def translation_matrix(far_index, far_count, trans_index, translators):
@@ -355,19 +374,20 @@
     boxes = currents.shape[1]
     reach = boxes // 2
     parts = lax.axis_size(AXES)
-    lower = passed_along(currents[:, boxes - reach :], AXES, 1)
-    upper = passed_along(currents[:, :reach], AXES, -1)
+    lower = [passed_along(currents[part, boxes - reach :], AXES, 1) for part in range(2)]
+    upper = [passed_along(currents[part, :reach], AXES, -1) for part in range(2)]
     cosine = jnp.cos(shift_angle)
     sine = jnp.sin(shift_angle)
     parent = upward(currents, radiate, interp, cosine, sine, parts)
-    parent, lower, upper, far_index, trans_index, translators = lax.optimization_barrier(
-        (parent, lower, upper, far_index, trans_index, translators)
+    parent, lower[0], upper[0], far_index, trans_index, translators = lax.optimization_barrier(
+        (parent, lower[0], upper[0], far_index, trans_index, translators)
     )
     by_direction = lax.all_to_all(parent, AXES, split_axis=0, concat_axis=0, tiled=True)
     matrix = wire_matrix(
         translation_matrix(far_index, far_count, trans_index, translators), parts
     )
     first = lax.axis_index(AXES) * boxes - reach
+    by_direction, lower[1], upper[1] = lax.optimization_barrier((by_direction, lower[1], upper[1]))
     translated = translate(by_direction, matrix)
     translated, near_count = lax.optimization_barrier((translated, near_count))
     near = near_products(lower, currents, upper, near_tiles, near_index, near_count, first)

time: 141 us -> 131 us (0.929)
  waiting for transfers between devices: 27.6 us -> 21.7 us
  starting transfers between devices: 37.3 us -> 32.4 us
  local copies, waits for them, and re-layouts: 6.15 us -> 7.82 us
    all_to_all x1, starting transfers between devices: 28.8 us -> 13.1 us  [local(): lax.all_to_all(parent, AXES, split_axis=0, concat_axis=0, tiled=True)]
    all_to_all x1, starting transfers between devices: 3.66 us -> 11.4 us  [local(): lax.all_to_all(translated, AXES, split_axis=0, concat_axis=0, tiled=True)]
    all_to_all x1, waiting for transfers between devices: 26 us -> 20.2 us  [local(): lax.all_to_all(parent, AXES, split_axis=0, concat_axis=0, tiled=True)]
    slice x1 -> x0, local copies, waits for them, and re-layouts: 4.02 us -> none  [local(): upper = passed_along(currents[:, :reach], AXES, -1)]
    squeeze x0 -> x1, local copies, waits for them, and re-layouts: none -> 3.66 us  [local(): currents[part, :reach]]
    ppermute x2 -> x4, starting transfers between devices: 4.8 us -> 8.03 us  [passed_along(): return lax.ppermute(value, axis, pairs)]
  transfers between devices with their start and end apart: 4 -> 6, of which waited for: 2 -> 2; matrix products, arithmetic and copies ran while one was open for 3% -> 5% of each run, Pallas kernels for 39% -> 41%
where the time goes in v3:
time: 131 us; the launch traced here: 130 us
  Pallas kernels  64.6 us (49%)
  starting transfers between devices  32.4 us (25%)
  waiting for transfers between devices  21.7 us (17%)
  local copies, waits for them, and re-layouts  7.82 us (6%)
  matrix products  3.25 us (2%)
    pallas_call x1, Pallas kernels, near_products(): pl.pallas_call(body, grid_spec=pltpu.PrefetchScalarGridSpec(num_scalar_pr...  34.5 us
    all_to_all x1, waiting for transfers between devices, local(): lax.all_to_all(parent, AXES, split_axis=0, concat_axis=0, tiled=True)  20.2 us
    all_to_all x1, starting transfers between devices, local(): lax.all_to_all(parent, AXES, split_axis=0, concat_axis=0, tiled=True)  13.1 us
    pallas_call x1, Pallas kernels, upward(): pl.pallas_call(body, grid=(8 + parents,), in_specs=[pl.BlockSpec((2, pare...  11.5 us
    all_to_all x1, starting transfers between devices, local(): lax.all_to_all(translated, AXES, split_axis=0, concat_axis=0, tiled=True)  11.4 us
    ppermute x4, starting transfers between devices, passed_along(): return lax.ppermute(value, axis, pairs)  8.03 us
    pallas_call x1, Pallas kernels, downward(): pl.pallas_call(body, grid=(parents,), in_specs=[in_spec, pl.BlockSpec((2,...  7.88 us
    pallas_call x1, Pallas kernels, wire_matrix(): pl.pallas_call(body, grid=(share,), in_specs=[pl.BlockSpec((1, total, tot...  7.16 us
  transfers between devices with their start and end apart: 6, of which 2 were waited for; matrix products, arithmetic and copies ran while one was open for 5% of the time, Pallas kernels for 41%

profile of v3, /device:TPU:0, one launch (start us, length us, event | category | flops | bytes accessed | tf_op | source)
XLA Modules:
  0.0 130.3 jit_solution(5308598205328422536)
XLA Ops:
  0.0 0.0 copy-start.9
  0.0 3.7 %slice_bitcast_fusion = (bf16[12,128,256]{2,1,0:T(8,128)(2,1)}, bf16[12,128,256]{2,1,0:T(8,128)(2,1)}, bf16[12,128,256]{2,1,0:T(8,128)(2,1)}, bf16[12,128,256]{2,1,0:T(8,128)(2,1)}) fusion(bf16[2,24,128,256]{3,2,1,0:T(8,128)(2,1)} %cur_ref.1), kind=kLoop, calls=%fused_computation.10 | loop fusion | bytes 6291456 | tf_op jit(solution)/shard_map/squeeze | solution.py:378
  3.7 2.4 %collective-permute-start = (bf16[12,128,256]{2,1,0:T(8,128)(2,1)}, bf16[12,128,256]{2,1,0:T(8,128)(2,1)S(1)}, u32[]{:S(2)}, u32[]{:S(2)}) collective-permute-start(bf16[12,128,256]{2,1,0:T(8,128)(2,1)} %get-tuple-element.30), channel_id=1, source_target_pairs={{0,1},{1,2},{2,3},{3,4},{4,5},{5,6},{6,7},{7,8},{8,9},{9,10},{10,1... | collective-permute-start | bytes 2359304 | tf_op jit(solution)/shard_map/ppermute | solution.py:15
  6.1 1.3 collective-permute-start.1
  7.4 0.0 copy-done.9
  7.4 0.1 fusion.17
  7.5 0.1 copy.29.cos_ref
  7.6 0.1 copy.30.sin_ref
  7.7 0.0 copy-done.2
  7.7 0.0 copy-done.1
  7.7 11.5 %upward.1 = bf16[32,2,3,16,256]{4,3,2,1,0:T(8,128)(2,1)} custom-call(bf16[2,3,8,128,256]{4,3,2,1,0:T(8,128)(2,1)} %bitcast.35, bf16[3,8,2,128,128]{4,3,2,1,0:T(8,128)(2,1)S(1)} %bitcast.34, bf16[512,128]{1,0:T(8,128)(2,1)S(1)} %copy-done.1, f32[512,8]{1,0:T(8,128)S(1)} %copy.29.cos_ref, f32[512,8]{1,0:T(8,128)S(1)} %copy.30.sin_ref), custom_call_target="tpu_custom_call" | custom-call | flops 4026531840 | bytes 6291456 | tf_op jit(solution)/shard_map/upward/pallas_call | solution.py:84
  19.3 0.0 collective-permute-done.low_real
  19.3 0.0 copy-start.3
  19.3 0.0 collective-permute-done.1.up_real
  19.3 13.1 %all-to-all-start = ((bf16[32,2,3,16,256]{4,3,2,1,0:T(8,128)(2,1)}), bf16[32,2,3,16,256]{4,3,2,1,0:T(8,128)(2,1)S(1)}, u32[]{:S(2)}, u32[]{:S(2)}) async-start(bf16[32,2,3,16,256]{4,3,2,1,0:T(8,128)(2,1)} %upward.1), calls=%async_computation | async-start | bytes 3145728 | tf_op jit(solution)/shard_map/all_to_all | solution.py:385
  32.4 0.0 copy-start.8
  32.4 3.1 %collective-permute-start.2 = (bf16[12,128,256]{2,1,0:T(8,128)(2,1)}, bf16[12,128,256]{2,1,0:T(8,128)(2,1)}, u32[]{:S(2)}, u32[]{:S(2)}) collective-permute-start(bf16[12,128,256]{2,1,0:T(8,128)(2,1)} %get-tuple-element.28), channel_id=1, source_target_pairs={{0,1},{1,2},{2,3},{3,4},{4,5},{5,6},{6,7},{7,8},{8,9},{9,10},{10,1... | collective-permute-start | bytes 2359304 | tf_op jit(solution)/shard_map/ppermute | solution.py:15
  35.4 1.3 collective-permute-start.3
  36.8 0.1 copy.35.spread_ref
  37.0 0.0 copy-done.7
  37.0 0.0 copy-done.11
  37.0 0.1 copy.32
  37.1 0.1 eq.80
  37.2 0.0 copy-done.6
  37.2 1.1 fusion.1
  38.3 0.0 copy-done.3
  38.3 1.7 %reshape.177 = bf16[96,48,32]{1,0,2:T(8,128)(2,1)} reshape(bf16[4608,32]{0,1:T(8,128)(2,1)S(1)} %fusion.1) | data formatting | bytes 589824 | tf_op jit(solution)/shard_map/reshape | solution.py:220
  40.0 0.0 copy-done.8
  40.0 0.1 copy.31
  40.1 2.2 %fusion.3 = bf16[96,96,32]{1,2,0:T(8,128)(2,1)S(1)} fusion(s32[96,48]{1,0:T(8,128)S(1)} %copy.31, bf16[96,48,32]{1,0,2:T(8,128)(2,1)} %reshape.177), kind=kOutput, calls=%fused_computation.5 | convolution fusion | flops 28753920 | bytes 903168 | tf_op jit(solution)/shard_map/psx,psq->xpq/dot_general | solution.py:223
  42.3 0.3 copy.43
  42.6 7.2 %wire_matrix.1.mat_ref = bf16[16,192,192]{2,1,0:T(8,128)(2,1)S(1)} custom-call(bf16[32,96,96]{2,1,0:T(8,128)(2,1)S(1)} %bitcast.27, bf16[32,96,96]{2,1,0:T(8,128)(2,1)S(1)} %bitcast.28, bf16[2,192,96]{2,1,0:T(8,128)(2,1)S(1)} %copy.35.spread_ref, bf16[2,96,192]{2,1,0:T(8,128)(2,1)S(1)} %get-tuple-element.31.gather_ref), custom_call_target="tpu_custom_call" | custom-call | flops 226492416 | bytes 1769472 | tf_op jit(solution)/shard_map/wire_matrix/pallas_call | solution.py:247
  49.8 0.0 collective-permute-done.2.low_imag
  49.8 0.0 collective-permute-done.3.up_imag
  49.8 20.2 %all-to-all-done = bf16[32,2,3,16,256]{4,3,2,1,0:T(8,128)(2,1)S(1)} async-done(((bf16[32,2,3,16,256]{4,3,2,1,0:T(8,128)(2,1)}), bf16[32,2,3,16,256]{4,3,2,1,0:T(8,128)(2,1)S(1)}, u32[]{:S(2)}, u32[]{:S(2)}) %all-to-all-start) | async-done | bytes 1572896 | tf_op jit(solution)/shard_map/all_to_all | solution.py:385
  70.0 3.5 %translate.1 = bf16[3072,256]{1,0:T(8,128)(2,1)} custom-call(bf16[3072,256]{1,0:T(8,128)(2,1)S(1)} %bitcast.29, bf16[16,192,192]{2,1,0:T(8,128)(2,1)S(1)} %wire_matrix.1.mat_ref), custom_call_target="tpu_custom_call" | custom-call | tf_op jit(solution)/shard_map/translate/pallas_call | solution.py:279
  73.5 11.4 %all-to-all-start.1 = ((bf16[32,2,3,16,256]{4,3,2,1,0:T(8,128)(2,1)}), bf16[32,2,3,16,256]{4,3,2,1,0:T(8,128)(2,1)S(1)}, u32[]{:S(2)}, u32[]{:S(2)}) async-start(bf16[32,2,3,16,256]{4,3,2,1,0:T(8,128)(2,1)} %bitcast.12), calls=%async_computation.1 | async-start | bytes 3145728 | tf_op jit(solution)/shard_map/all_to_all | solution.py:394
  84.9 0.1 copy.37
  85.0 0.0 copy-done.10
  85.0 0.1 copy.36
  85.1 0.1 reshape.179.index_ref
  85.2 0.0 copy-done.5
  85.2 0.0 copy-start.4
  85.2 1.1 copy-done.4
  86.4 34.5 %near_products.1 = bf16[2,24,128,256]{3,2,1,0:T(8,128)(2,1)} custom-call(s32[216]{0:T(256)S(1)} %reshape.179.index_ref, s32[24]{0:T(128)S(1)} %copy-done.5, bf16[12,128,256]{2,1,0:T(8,128)(2,1)S(1)} %copy-done.4, bf16[12,128,256]{2,1,0:T(8,128)(2,1)} %collective-permute-done.2.low_imag, bf16[2,24,128,256]{3,2,1,0:T(8,128)(2,1)} %cur_ref.1, ...), custom_call_target="tpu_custom_call" | custom-call | flops 7247757312 | bytes 26738688 | tf_op jit(solution)/shard_map/near_products/pallas_call | solution.py:176
  120.9 1.5 %all-to-all-done.1.in_ref = bf16[32,2,3,16,256]{4,3,2,1,0:T(8,128)(2,1)S(1)} async-done(((bf16[32,2,3,16,256]{4,3,2,1,0:T(8,128)(2,1)}), bf16[32,2,3,16,256]{4,3,2,1,0:T(8,128)(2,1)S(1)}, u32[]{:S(2)}, u32[]{:S(2)}) %all-to-all-start.1) | async-done | bytes 1572896 | tf_op jit(solution)/shard_map/all_to_all | solution.py:394
  122.4 0.0 copy-done
  122.4 7.9 %downward.1 = bf16[2,3,8,128,256]{4,3,2,1,0:T(8,128)(2,1)} custom-call(bf16[32,2,3,16,256]{4,3,2,1,0:T(8,128)(2,1)S(1)} %all-to-all-done.1.in_ref, bf16[2,3,8,128,256]{4,3,2,1,0:T(8,128)(2,1)} %bitcast.36, bf16[3,8,2,128,128]{4,3,2,1,0:T(8,128)(2,1)S(1)} %bitcast.30, bf16[128,512]{1,0:T(8,128)(2,1)S(1)} %bitcast.31, f32[8,512]{1,0:T(8,128)S(1)} %get-tuple-element.34.cos_ref, ...), custom_call_target="tpu_custom_call" | custom-call | tf_op jit(solution)/shard_map/downward/pallas_call | solution.py:337
  (15 shorter events, 0.1 us)
Async XLA Ops:
  0.0 7.4 %copy-start.9 = (f32[8,512]{1,0:T(8,128)S(1)}, f32[8,512]{1,0:T(8,128)}, u32[]{:S(2)}) copy-start(f32[8,512]{1,0:T(8,128)} %param.19) | copy-start | bytes 49156
  0.0 7.7 %copy-start.2 = (bf16[24,2,128,128]{3,2,1,0:T(8,128)(2,1)S(1)}, bf16[24,2,128,128]{3,2,1,0:T(8,128)(2,1)}, u32[]{:S(2)}) copy-start(bf16[24,2,128,128]{3,2,1,0:T(8,128)(2,1)} %param.16) | copy-start | bytes 4718596
  0.0 7.7 %copy-start.1 = (bf16[512,128]{1,0:T(8,128)(2,1)S(1)}, bf16[512,128]{1,0:T(8,128)(2,1)}, u32[]{:S(2)}) copy-start(bf16[512,128]{1,0:T(8,128)(2,1)} %interp_ref.1) | copy-start | bytes 393220
  3.7 15.6 %collective-permute-start = (bf16[12,128,256]{2,1,0:T(8,128)(2,1)}, bf16[12,128,256]{2,1,0:T(8,128)(2,1)S(1)}, u32[]{:S(2)}, u32[]{:S(2)}) collective-permute-start(bf16[12,128,256]{2,1,0:T(8,128)(2,1)} %get-tuple-element.30), channel_id=1, source_target_pairs={{0,1},{1,2},{2,3},{3,4},{4,5},{5,6},{6,7},{7,8},{8,9},{9,10},{10,1... | collective-permute-start | bytes 2359304 | tf_op jit(solution)/shard_map/ppermute | solution.py:15
  6.1 13.2 %collective-permute-start.1 = (bf16[12,128,256]{2,1,0:T(8,128)(2,1)}, bf16[12,128,256]{2,1,0:T(8,128)(2,1)}, u32[]{:S(2)}, u32[]{:S(2)}) collective-permute-start(bf16[12,128,256]{2,1,0:T(8,128)(2,1)} %get-tuple-element.29), channel_id=1, source_target_pairs={{1,0},{2,1},{3,2},{4,3},{5,4},{6,5},{7,6},{8,7},{9,8},{10,9},{11,1... | collective-permute-start | bytes 2359304 | tf_op jit(solution)/shard_map/ppermute | solution.py:15
  19.3 17.7 %copy-start.7 = (s32[96,48]{0,1:T(8,128)S(1)}, s32[96,48]{0,1:T(8,128)}, u32[]{:S(2)}) copy-start(s32[96,48]{0,1:T(8,128)} %param.22) | copy-start | bytes 55300
  19.3 17.7 %copy-start.11 = (s32[96]{0:T(128)S(1)}, s32[96]{0:T(128)}, u32[]{:S(2)}) copy-start(s32[96]{0:T(128)} %param.21) | copy-start | bytes 1156
  19.3 17.9 %copy-start.6 = (f32[316,2,16]{0,2,1:T(8,128)S(1)}, f32[316,2,16]{0,2,1:T(8,128)}, u32[]{:S(2)}) copy-start(f32[316,2,16]{0,2,1:T(8,128)} %param.23) | copy-start | bytes 121348
  19.3 19.0 %copy-start.3 = (bf16[12,128,256]{2,1,0:T(8,128)(2,1)}, bf16[12,128,256]{2,1,0:T(8,128)(2,1)S(1)}, u32[]{:S(2)}) copy-start(bf16[12,128,256]{2,1,0:T(8,128)(2,1)S(1)} %collective-permute-done.low_real) | copy-start | bytes 2359300
  19.3 50.7 %all-to-all-start = ((bf16[32,2,3,16,256]{4,3,2,1,0:T(8,128)(2,1)}), bf16[32,2,3,16,256]{4,3,2,1,0:T(8,128)(2,1)S(1)}, u32[]{:S(2)}, u32[]{:S(2)}) async-start(bf16[32,2,3,16,256]{4,3,2,1,0:T(8,128)(2,1)} %upward.1), calls=%async_computation | async-start | bytes 3145728 | tf_op jit(solution)/shard_map/all_to_all | solution.py:385
  32.4 7.6 %copy-start.8 = (s32[96,48]{0,1:T(8,128)S(1)}, s32[96,48]{0,1:T(8,128)}, u32[]{:S(2)}) copy-start(s32[96,48]{0,1:T(8,128)} %param.20) | copy-start | bytes 55300
  32.4 17.4 %collective-permute-start.2 = (bf16[12,128,256]{2,1,0:T(8,128)(2,1)}, bf16[12,128,256]{2,1,0:T(8,128)(2,1)}, u32[]{:S(2)}, u32[]{:S(2)}) collective-permute-start(bf16[12,128,256]{2,1,0:T(8,128)(2,1)} %get-tuple-element.28), channel_id=1, source_target_pairs={{0,1},{1,2},{2,3},{3,4},{4,5},{5,6},{6,7},{7,8},{8,9},{9,10},{10,1... | collective-permute-start | bytes 2359304 | tf_op jit(solution)/shard_map/ppermute | solution.py:15
  35.4 14.3 %collective-permute-start.3 = (bf16[12,128,256]{2,1,0:T(8,128)(2,1)}, bf16[12,128,256]{2,1,0:T(8,128)(2,1)}, u32[]{:S(2)}, u32[]{:S(2)}) collective-permute-start(bf16[12,128,256]{2,1,0:T(8,128)(2,1)} %get-tuple-element.27), channel_id=1, source_target_pairs={{1,0},{2,1},{3,2},{4,3},{5,4},{6,5},{7,6},{8,7},{9,8},{10,9},{11,1... | collective-permute-start | bytes 2359304 | tf_op jit(solution)/shard_map/ppermute | solution.py:15
  73.5 11.5 %copy-start.10 = (s32[24,9]{0,1:T(8,128)S(1)}, s32[24,9]{0,1:T(8,128)}, u32[]{:S(2)}) copy-start(s32[24,9]{0,1:T(8,128)} %param.14) | copy-start | bytes 2596
  73.5 11.7 %copy-start.5 = (s32[24]{0:T(128)S(1)}, s32[24]{0:T(128)}, u32[]{:S(2)}) copy-start(s32[24]{0:T(128)} %count_ref) | copy-start | bytes 292
  73.5 48.9 %all-to-all-start.1 = ((bf16[32,2,3,16,256]{4,3,2,1,0:T(8,128)(2,1)}), bf16[32,2,3,16,256]{4,3,2,1,0:T(8,128)(2,1)S(1)}, u32[]{:S(2)}, u32[]{:S(2)}) async-start(bf16[32,2,3,16,256]{4,3,2,1,0:T(8,128)(2,1)} %bitcast.12), calls=%async_computation.1 | async-start | bytes 3145728 | tf_op jit(solution)/shard_map/all_to_all | solution.py:394
  85.2 1.1 copy-start.4
  86.4 36.0 %copy-start = (bf16[24,2,128,128]{3,2,1,0:T(8,128)(2,1)S(1)}, bf16[24,2,128,128]{3,2,1,0:T(8,128)(2,1)}, u32[]{:S(2)}) copy-start(bf16[24,2,128,128]{3,2,1,0:T(8,128)(2,1)} %param.17) | copy-start | bytes 4718596
